TPU v7x, 128 devices: a whole 4x4x4 slice. The times are simulated.
128 devices in a mesh: gx: 8 (over y, z_lo), gy: 16 (over z_hi, x, core).
Axes of the slice: x: 4, y: 4, z: 4 (z_hi: 2, z_lo: 2; z = z_hi * 2 + z_lo), core: 2. Of those that a mesh axis runs over, the one named last changes fastest.
Arguments:
- samples: bfloat16 [512, 1024, 1024], P('gx', 'gy'), may hold values from -6 to 6
- box_labels: int32 [16], replicated, may hold values from 0 to 15, each once
Outputs:
- coefficients: float32 [8, 16, 2048, 1024], P('gx', 'gy')
Inputs may be any that keep to these rules, and one draw needn't show every extreme that they name: `box_labels`: each of the 16 box labels appears exactly once.
All inputs are finite; a program needn't handle non-finite values.
Results may differ from a plain program's by a relative error of at most 0.0029.
Values sent between devices are 32-bit elements; how exact they have to be, the bound alone decides.
A program may use at most 128 MiB of HBM per device.

v0:
```python
import math

import jax
import jax.numpy as jnp
from jax import lax
from jax.sharding import PartitionSpec as P

N = 16384
FBY = 4
FB = 16
Q1 = 8
Q2 = 16


def swapped(x, axis, distance):
    return lax.ppermute(x, axis, [(i, i ^ 1 << distance) for i in range(lax.axis_size(axis))])


def cheb_nodes(points):
    counter = jnp.arange(points, dtype=jnp.float32)
    return jnp.cos(jnp.pi * (2.0 * counter + 1.0) / (2.0 * points))


def lagrange_table(cheb_points, targets):
    points = cheb_points.shape[0]
    diagonal_mask = jnp.eye(points, dtype=bool)[None, :, :]
    numerator = targets[:, None, None] - cheb_points[None, None, :]
    denominator = cheb_points[None, :, None] - cheb_points[None, None, :]
    factors = jnp.where(diagonal_mask, 1.0, numerator / jnp.where(diagonal_mask, 1.0, denominator))
    return jnp.prod(factors, axis=2)


def level_matrix(points, box_ratio, source_side, child_half):
    cheb_points = cheb_nodes(points)
    side_value = jnp.asarray(source_side).astype(jnp.float32)
    child_value = jnp.asarray(child_half).astype(jnp.float32)
    targets = child_value - 0.5 + 0.5 * cheb_points
    weights = lagrange_table(cheb_points, targets)
    phase_turns = (
        (child_value - 0.5) * 0.5 + 0.25 * cheb_points[:, None] - 0.5 * cheb_points[None, :]
    ) * (box_ratio * (side_value - 0.5) * 0.5)
    radians = 2.0 * jnp.pi * phase_turns
    return weights * (jnp.cos(radians) + jnp.sin(radians))


def initial_coefficients(sample_block, labels, corner_x, corner_y):
    size_x, size_y, records = sample_block.shape
    flattened = sample_block.reshape(size_x * size_y, records)
    group_size = min(FB, max(1, 512 // (Q1 * Q2)))
    width_x = N // (2 * size_x)
    width_y = N // (2 * size_y)
    nodes_x = cheb_nodes(Q1)
    nodes_y = cheb_nodes(Q2)
    offset_x = jnp.arange(size_x, dtype=jnp.float32)
    offset_y = jnp.arange(size_y, dtype=jnp.float32)

    def one_group(labels_group):
        label_x = labels_group // FBY
        label_y = labels_group % FBY
        centre_x = label_x * width_x + width_x // 2
        centre_y = label_y * width_y + width_y // 2
        corner_turns = ((corner_x * centre_x + corner_y * centre_y) % N).astype(jnp.float32)
        points_x = centre_x.astype(jnp.float32)[:, None] + 0.5 * width_x * nodes_x[None, :]
        points_y = centre_y.astype(jnp.float32)[:, None] + 0.5 * width_y * nodes_y[None, :]
        phase_turns = (
            corner_turns[:, None, None, None, None]
            + points_x[:, :, None, None, None] * offset_x[None, None, None, :, None]
            + points_y[:, None, :, None, None] * offset_y[None, None, None, None, :]
        ) / N
        radians = 2.0 * jnp.pi * phase_turns
        cas_table = (jnp.cos(radians) + jnp.sin(radians)).astype(jnp.bfloat16)
        cas_table = cas_table.reshape(labels_group.shape[0] * Q1 * Q2, size_x * size_y)
        return jnp.dot(cas_table, flattened, preferred_element_type=jnp.float32)

    blocks = lax.map(one_group, labels.reshape(FB // group_size, group_size))
    norm_scale = 1.0 / math.sqrt(size_x * size_y)
    return (blocks * norm_scale).reshape(FB, Q1, Q2, records)


def along_first(matrix, coeffs):
    return jnp.einsum("pq,aqjv->apjv", matrix, coeffs, precision=lax.Precision.HIGHEST)


def along_second(matrix, coeffs):
    return jnp.einsum("pq,aiqv->aipv", matrix, coeffs, precision=lax.Precision.HIGHEST)


def local(samples, box_labels):
    size_x = lax.axis_size("gx")
    size_y = lax.axis_size("gy")
    device_x = lax.axis_index("gx")
    device_y = lax.axis_index("gy")
    rows_box = samples.shape[0]
    cols_box = samples.shape[1]
    initial = initial_coefficients(samples, box_labels, device_x * rows_box, device_y * cols_box)
    ratio_x = 2.0 * rows_box * (N // (2 * rows_box)) / N
    ratio_y = 2.0 * cols_box * (N // (2 * cols_box)) / N
    side_x = device_x // (size_x // 2)
    side_y = device_y // (size_y // 2)
    bit_x = size_x.bit_length() - 2
    bit_y = size_y.bit_length() - 2
    kept_x = level_matrix(Q1, ratio_x, side_x, side_x)
    kept_y = level_matrix(Q2, ratio_y, side_y, side_y)
    outgoing = along_first(level_matrix(Q1, ratio_x, side_x, 1 - side_x), initial)
    merged_x = along_first(kept_x, initial) + swapped(outgoing, "gx", bit_x)
    outgoing = along_second(level_matrix(Q2, ratio_y, side_y, 1 - side_y), merged_x)
    merged_y = along_second(kept_y, merged_x) + swapped(outgoing, "gy", bit_y)
    return merged_y.reshape(1, 1, FB * Q1 * Q2, merged_y.shape[-1])


def solution(mesh):
    in_specs = (P("gx", "gy", None), P())
    out_specs = P("gx", "gy", None, None)
    return jax.shard_map(local, mesh=mesh, in_specs=in_specs, out_specs=out_specs, check_vma=False)
```

profile of v0, /device:TPU:1, one launch (start us, length us, event | category | flops | bytes accessed | tf_op | source)
XLA Modules:
  0.0 779.5 jit_solution(15447970518734791270)
XLA Ops:
  0.2 0.7 reshape.544
  0.9 339.6 %while.16 = (s32[]{:T(128)}, f32[4,512,1024]{2,1,0:T(8,128)}, s32[]{:T(128)}, s32[4,4]{1,0:T(4,128)S(1)}, s32[]{:T(128)}, /*index=5*/bf16[4096,1024]{1,0:T(8,128)(2,1)}, s32[]{:T(128)}) while((s32[]{:T(128)}, f32[4,512,1024]{2,1,0:T(8,128)}, s32[]{:T(128)}, s32[4,4]{1,0:T(4,128)S(1)}, s32[]{:T(128)}, ...), condition=%wide.region_1.2_spmd.clone.clone, body=%wide.region_0.1_spmd.clone.clone.sunk | while | flops 4303364608 | bytes 27313864 | solution.py:75
  1.4 61.9 %add_convert_fusion.2 = bf16[4,8,16,64,64]{4,3,2,1,0:T(8,128)(2,1)} fusion(f32[4,16,64]{2,1,0:T(8,128)S(1)} %iota_multiply_fusion.3, f32[4,8,64]{2,1,0:T(8,128)S(1)} %fusion.99), kind=kLoop, calls=%fused_computation.3.clone.1 | loop fusion | flops 8388608 | bytes 4218880 | tf_op jit(solution)/shard_map/convert
  63.3 12.0 %add.639 = bf16[512,4096]{1,0:T(8,128)(2,1)} reshape(bf16[4,8,16,64,64]{4,3,2,1,0:T(8,128)(2,1)} %add_convert_fusion.2) | data formatting | bytes 8388608 | tf_op jit(solution)/shard_map/while/body/eval_jaxpr/add | solution.py:71
  75.4 10.5 %bitcast_dynamic-update-slice_fusion.2 = f32[4,512,1024]{2,1,0:T(8,128)} fusion(f32[4,512,1024]{2,1,0:T(8,128)} %get-tuple-element.307, s32[]{:T(128)} %get-tuple-element.306, bf16[512,4096]{1,0:T(8,128)(2,1)} %add.639, bf16[4096,1024]{1,0:T(8,128)(2,1)} %get-tuple-element.318), kind=kOutput, calls=%fused_computation.4.clone.1 | convolution fusion | flops 4294967296 | bytes 14680576 | tf_op jit(solution)/shard_map/while/body/eval_jaxpr/dot_general | solution.py:73
  86.3 61.9 %add_convert_fusion.2 = bf16[4,8,16,64,64]{4,3,2,1,0:T(8,128)(2,1)} fusion(f32[4,16,64]{2,1,0:T(8,128)S(1)} %iota_multiply_fusion.3, f32[4,8,64]{2,1,0:T(8,128)S(1)} %fusion.99), kind=kLoop, calls=%fused_computation.3.clone.1 | loop fusion | flops 8388608 | bytes 4218880 | tf_op jit(solution)/shard_map/convert
  148.2 12.0 %add.639 = bf16[512,4096]{1,0:T(8,128)(2,1)} reshape(bf16[4,8,16,64,64]{4,3,2,1,0:T(8,128)(2,1)} %add_convert_fusion.2) | data formatting | bytes 8388608 | tf_op jit(solution)/shard_map/while/body/eval_jaxpr/add | solution.py:71
  160.3 10.5 %bitcast_dynamic-update-slice_fusion.2 = f32[4,512,1024]{2,1,0:T(8,128)} fusion(f32[4,512,1024]{2,1,0:T(8,128)} %get-tuple-element.307, s32[]{:T(128)} %get-tuple-element.306, bf16[512,4096]{1,0:T(8,128)(2,1)} %add.639, bf16[4096,1024]{1,0:T(8,128)(2,1)} %get-tuple-element.318), kind=kOutput, calls=%fused_computation.4.clone.1 | convolution fusion | flops 4294967296 | bytes 14680576 | tf_op jit(solution)/shard_map/while/body/eval_jaxpr/dot_general | solution.py:73
  171.2 61.9 %add_convert_fusion.2 = bf16[4,8,16,64,64]{4,3,2,1,0:T(8,128)(2,1)} fusion(f32[4,16,64]{2,1,0:T(8,128)S(1)} %iota_multiply_fusion.3, f32[4,8,64]{2,1,0:T(8,128)S(1)} %fusion.99), kind=kLoop, calls=%fused_computation.3.clone.1 | loop fusion | flops 8388608 | bytes 4218880 | tf_op jit(solution)/shard_map/convert
  233.1 12.0 %add.639 = bf16[512,4096]{1,0:T(8,128)(2,1)} reshape(bf16[4,8,16,64,64]{4,3,2,1,0:T(8,128)(2,1)} %add_convert_fusion.2) | data formatting | bytes 8388608 | tf_op jit(solution)/shard_map/while/body/eval_jaxpr/add | solution.py:71
  245.2 10.5 %bitcast_dynamic-update-slice_fusion.2 = f32[4,512,1024]{2,1,0:T(8,128)} fusion(f32[4,512,1024]{2,1,0:T(8,128)} %get-tuple-element.307, s32[]{:T(128)} %get-tuple-element.306, bf16[512,4096]{1,0:T(8,128)(2,1)} %add.639, bf16[4096,1024]{1,0:T(8,128)(2,1)} %get-tuple-element.318), kind=kOutput, calls=%fused_computation.4.clone.1 | convolution fusion | flops 4294967296 | bytes 14680576 | tf_op jit(solution)/shard_map/while/body/eval_jaxpr/dot_general | solution.py:73
  256.1 61.9 %add_convert_fusion.2 = bf16[4,8,16,64,64]{4,3,2,1,0:T(8,128)(2,1)} fusion(f32[4,16,64]{2,1,0:T(8,128)S(1)} %iota_multiply_fusion.3, f32[4,8,64]{2,1,0:T(8,128)S(1)} %fusion.99), kind=kLoop, calls=%fused_computation.3.clone.1 | loop fusion | flops 8388608 | bytes 4218880 | tf_op jit(solution)/shard_map/convert
  318.0 12.0 %add.639 = bf16[512,4096]{1,0:T(8,128)(2,1)} reshape(bf16[4,8,16,64,64]{4,3,2,1,0:T(8,128)(2,1)} %add_convert_fusion.2) | data formatting | bytes 8388608 | tf_op jit(solution)/shard_map/while/body/eval_jaxpr/add | solution.py:71
  330.1 10.5 %bitcast_dynamic-update-slice_fusion.2 = f32[4,512,1024]{2,1,0:T(8,128)} fusion(f32[4,512,1024]{2,1,0:T(8,128)} %get-tuple-element.307, s32[]{:T(128)} %get-tuple-element.306, bf16[512,4096]{1,0:T(8,128)(2,1)} %add.639, bf16[4096,1024]{1,0:T(8,128)(2,1)} %get-tuple-element.318), kind=kOutput, calls=%fused_computation.4.clone.1 | convolution fusion | flops 4294967296 | bytes 14680576 | tf_op jit(solution)/shard_map/while/body/eval_jaxpr/dot_general | solution.py:73
  340.6 4.4 broadcast_multiply_fusion
  345.4 13.9 %fusion.20 = f32[16,8,16,1024]{3,1,2,0:T(8,128)} fusion(f32[16,8,16,1024]{3,2,1,0:T(8,128)S(1)} %bitcast.60, f32[8,8]{1,0:T(8,128)S(1)} %get-tuple-element.226, f32[8]{0:T(128)S(1)} %get-tuple-element.250, f32[]{:T(128)S(6)} %mul.443, f32[8]{0:T(128)S(1)} %get-tuple-element.251), kind=kOutput, calls=%fused_computation.39 | convolution fusion | flops 201326912 | bytes 16777540 | tf_op jit(solution)/shard_map/pq,aqjv->apjv/dot_general | solution.py:81
  359.3 3.7 collective-permute-start
  363.3 0.6 fusion.28
  363.9 179.3 %collective-permute-done = f32[16,8,16,1024]{3,1,2,0:T(8,128)} collective-permute-done((f32[16,8,16,1024]{3,1,2,0:T(8,128)}, f32[16,8,16,1024]{3,1,2,0:T(8,128)}, u32[]{:S(2)}, u32[]{:S(2)}) %collective-permute-start) | collective-permute-done | bytes 8388640 | tf_op jit(solution)/shard_map/ppermute | solution.py:16
  543.2 21.2 %bitcast_add_fusion.1 = f32[16,8,16,1024]{3,1,2,0:T(8,128)S(1)} fusion(f32[16,8,16,1024]{3,1,2,0:T(8,128)} %collective-permute-done, f32[16,8,16,1024]{3,2,1,0:T(8,128)} %bitcast.61, f32[8,8]{1,0:T(8,128)S(1)} %get-tuple-element.225, f32[]{:T(128)S(6)} %mul.443, f32[8]{0:T(128)S(1)} %get-tuple-element.251, f32[8]{0:T(128)S(1)} %multiply_add_fusion.4), kind=kOutput, calls=%fused_computation.29 | convolution fusion | flops 203424064 | bytes 25166148 | tf_op jit(solution)/shard_map/pq,aqjv->apjv/dot_general | solution.py:81
  564.4 17.0 %fusion.23 = f32[16,8,16,1024]{3,2,1,0:T(8,128)S(1)} fusion(f32[16,8,16,1024]{3,1,2,0:T(8,128)S(1)} %bitcast_add_fusion.1, f32[16,16]{1,0:T(8,128)S(1)} %get-tuple-element.224, f32[16]{0:T(128)S(1)} %get-tuple-element.254, f32[]{:T(128)S(6)} %mul.454, f32[16]{0:T(128)S(1)} %get-tuple-element.255), kind=kOutput, calls=%fused_computation.40 | convolution fusion | flops 402654464 | bytes 16778372 | tf_op jit(solution)/shard_map/pq,aiqv->aipv/dot_general | solution.py:85
  581.5 3.7 collective-permute-start.1
  585.2 179.2 %collective-permute-done.1 = f32[16,8,16,1024]{3,2,1,0:T(8,128)S(1)} collective-permute-done((f32[16,8,16,1024]{3,2,1,0:T(8,128)S(1)}, f32[16,8,16,1024]{3,2,1,0:T(8,128)S(1)}, u32[]{:S(2)}, u32[]{:S(2)}) %collective-permute-start.1) | collective-permute-done | bytes 8388640 | tf_op jit(solution)/shard_map/ppermute | solution.py:16
  764.4 14.6 %bitcast_add_fusion = f32[16,8,16,1024]{3,2,1,0:T(8,128)} fusion(f32[16,8,16,1024]{3,2,1,0:T(8,128)S(1)} %collective-permute-done.1, f32[16,8,16,1024]{3,1,2,0:T(8,128)S(1)} %bitcast_add_fusion.1, f32[16,16]{1,0:T(8,128)S(1)} %get-tuple-element.223, f32[]{:T(128)S(6)} %mul.454, f32[16]{0:T(128)S(1)} %get-tuple-element.255, f32[16]{0:T(128)S(1)} %multiply_add_fusion.2), kind=kOutput, calls=%fused_computation.28 | convolution fusion | flops 404751616 | bytes 25166980 | tf_op jit(solution)/shard_map/pq,aiqv->aipv/dot_general | solution.py:85
  (52 shorter events, 2.7 us)
Async XLA Ops:
  344.9 14.4 %copy-start = (f32[4,512,1024]{2,1,0:T(8,128)}, f32[4,512,1024]{2,1,0:T(8,128)S(1)}, u32[]{:S(2)}) copy-start(f32[4,512,1024]{2,1,0:T(8,128)S(1)} %broadcast_multiply_fusion) | copy-start | bytes 25165828
  359.3 184.0 %collective-permute-start = (f32[16,8,16,1024]{3,1,2,0:T(8,128)}, f32[16,8,16,1024]{3,1,2,0:T(8,128)}, u32[]{:S(2)}, u32[]{:S(2)}) collective-permute-start(f32[16,8,16,1024]{3,1,2,0:T(8,128)} %fusion.20), channel_id=1, source_target_pairs={{0,64},{16,80},{32,96},{48,112},{64,0},{80,16},{96,32},{112,48},{1... | collective-permute-start | bytes 25165832 | tf_op jit(solution)/shard_map/ppermute | solution.py:16
  581.5 182.9 %collective-permute-start.1 = (f32[16,8,16,1024]{3,2,1,0:T(8,128)S(1)}, f32[16,8,16,1024]{3,2,1,0:T(8,128)S(1)}, u32[]{:S(2)}, u32[]{:S(2)}) collective-permute-start(f32[16,8,16,1024]{3,2,1,0:T(8,128)S(1)} %fusion.23), channel_id=1, source_target_pairs={{0,8},{1,9},{2,10},{3,11},{4,12},{5,13},{6,14},{7,15},{8,0},{9,1},... | collective-permute-start | bytes 25165832 | tf_op jit(solution)/shard_map/ppermute | solution.py:16
where the time goes:
time: 788 us; the launch traced here: 779 us
  waiting for transfers between devices  358 us (45%)
  other arithmetic  255 us (32%)
  matrix products  109 us (14%)
  local copies, waits for them, and re-layouts  48.9 us (6%)
    ppermute x2, waiting for transfers between devices, swapped(): lax.ppermute(x, axis, [(i, i ^ 1 << distance) for i in range(lax.axis_siz...  358 us
    another operation x4, other arithmetic  248 us
    add x4, local copies, waits for them, and re-layouts, one_group(): cas_table = (jnp.cos(radians) + jnp.sin(radians)).astype(jnp.bfloat16)  48.2 us
    dot_general x4, matrix products, one_group(): return jnp.dot(cas_table, flattened, preferred_element_type=jnp.float32)  41.9 us
    dot_general x2, matrix products, along_first(): jnp.einsum('pq,aqjv->apjv', matrix, coeffs, precision=lax.Precision.HIGHEST)  35.1 us
    dot_general x2, matrix products, along_second(): jnp.einsum('pq,aiqv->aipv', matrix, coeffs, precision=lax.Precision.HIGHEST)  31.6 us
  transfers between devices with their start and end apart: 2, of which 2 were waited for; matrix products, arithmetic and copies ran while one was open for 0% of the time, Pallas kernels for 0%

commit v1 on v0

v1 whole, which is shorter than its diff:
```python
import functools
import math

import jax
import jax.numpy as jnp
import numpy as np
from jax import lax
from jax.experimental import pallas as pl
from jax.experimental.pallas import tpu as pltpu
from jax.sharding import PartitionSpec as P

N = 16384
FBY = 4
FB = 16
Q1 = 8
Q2 = 16
Q = Q1 * Q2
LANES = 256
GROUPS = (1, 2, 4, 5, 3, 1)
VMEM = 48 << 20


def cheb_nodes(points):
    return np.cos(np.pi * (2.0 * np.arange(points) + 1.0) / (2.0 * points))


def level_matrix(points, box_ratio, side, child):
    nodes = cheb_nodes(points)
    targets = child - 0.5 + 0.5 * nodes
    weights = np.ones((points, points))
    for m in range(points):
        for other in range(points):
            if other != m:
                weights[:, m] *= (targets - nodes[other]) / (nodes[m] - nodes[other])
    turns = ((child - 0.5) * 0.5 + 0.25 * nodes[:, None] - 0.5 * nodes[None, :]) * (box_ratio * (side - 0.5) * 0.5)
    radians = 2.0 * np.pi * turns
    return weights * (np.cos(radians) + np.sin(radians))


def level_tables(points, box_ratio, spread, scale):
    both = np.stack(
        [
            np.concatenate([spread(level_matrix(points, box_ratio, s, c)) for c in (s, 1 - s)], axis=0)
            for s in (0, 1)
        ]
    )
    both = (both * scale).astype(np.float32)
    high = both.astype(jnp.bfloat16)
    low = (both - high.astype(np.float32)).astype(jnp.bfloat16)
    return jnp.asarray(high), jnp.asarray(low)


def product(high, low, value):
    value_high = value.astype(jnp.bfloat16)
    value_low = (value - value_high.astype(jnp.float32)).astype(jnp.bfloat16)
    dot = functools.partial(jnp.dot, preferred_element_type=jnp.float32)
    return dot(high, value_high) + (dot(low, value_high) + dot(high, value_low))


def node_column(points):
    counter = lax.broadcasted_iota(jnp.int32, (points, 1), 0).astype(jnp.float32)
    return jnp.cos(jnp.pi * (2.0 * counter + 1.0) / (2.0 * points))


def first_kernel(first_slot, slots, size_x, size_y, labels, place, x_ref, high_ref, low_ref, out_ref, kept_ref, spread_ref, cos_ref, sin_ref, table_ref):
    width_x, width_y = N // (2 * size_x), N // (2 * size_y)
    samples_box = size_x * size_y

    @pl.when(pl.program_id(0) == 0)
    def _():
        owner = lax.broadcasted_iota(jnp.int32, (size_x, samples_box), 1) // size_y
        row = lax.broadcasted_iota(jnp.int32, (size_x, samples_box), 0)
        spread_ref[...] = (owner == row).astype(jnp.float32).astype(jnp.bfloat16)
        steps_x = lax.broadcasted_iota(jnp.int32, (Q1, size_x), 1).astype(jnp.float32)
        steps_y = (lax.broadcasted_iota(jnp.int32, (Q2, 2 * size_y), 1) % size_y).astype(jnp.float32)
        nodes_x, nodes_y = node_column(Q1), node_column(Q2)

        def build(slot, _):
            label = labels[first_slot + slot]
            centre_x = (label // FBY) * width_x + width_x // 2
            centre_y = (label % FBY) * width_y + width_y // 2
            corner = ((place[0] * centre_x + place[1] * centre_y) % N).astype(jnp.float32)
            points_x = centre_x.astype(jnp.float32) + 0.5 * width_x * nodes_x
            points_y = centre_y.astype(jnp.float32) + 0.5 * width_y * nodes_y
            angle_x = 2.0 * jnp.pi * ((corner + points_x * steps_x) / N)
            angle_y = 2.0 * jnp.pi * ((points_y * steps_y) / N)
            cos_y, sin_y = jnp.cos(angle_y), jnp.sin(angle_y)
            plus_y, minus_y = cos_y + sin_y, cos_y - sin_y
            parts = jnp.concatenate([jnp.cos(angle_x), jnp.sin(angle_x)], axis=0)
            parts_high = parts.astype(jnp.bfloat16).astype(jnp.float32)
            stacked = jnp.concatenate([parts_high, parts - parts_high], axis=0).astype(jnp.bfloat16)
            wide = jnp.dot(stacked, spread_ref[...], preferred_element_type=jnp.float32)
            cos_ref[...] = wide[:Q1] + wide[2 * Q1 : 3 * Q1]
            sin_ref[...] = wide[Q1 : 2 * Q1] + wide[3 * Q1 :]
            for at in range(0, samples_box, 2 * size_y):
                for i in range(Q1):
                    cos_x = cos_ref[i : i + 1, at : at + 2 * size_y]
                    sin_x = sin_ref[i : i + 1, at : at + 2 * size_y]
                    table_ref[slot, i * Q2 : (i + 1) * Q2, at : at + 2 * size_y] = (
                        cos_x * plus_y + sin_x * minus_y
                    ).astype(jnp.bfloat16)
            return 0

        lax.fori_loop(0, slots, build, 0)

    side = place[2]

    def apply(slot, _):
        initial = jnp.dot(table_ref[slot], x_ref[...].reshape(samples_box, LANES), preferred_element_type=jnp.float32)
        both = product(high_ref[side], low_ref[side], initial)
        kept_ref[slot] = both[:Q]
        out_ref[slot] = both[Q:]
        return 0

    lax.fori_loop(0, slots, apply, 0)


def first(labels, place, samples, tables, first_slot, slots, half):
    size_x, size_y, records = samples.shape
    samples_box = size_x * size_y
    blocks = records // 2 // LANES
    smem = pl.BlockSpec(memory_space=pltpu.SMEM)
    whole = pl.BlockSpec((2, 2 * Q, Q), lambda j: (0, 0, 0))
    made = pl.BlockSpec((slots, Q, LANES), lambda j: (0, 0, j))
    shape = jax.ShapeDtypeStruct((slots, Q, records // 2), jnp.float32)
    return pl.pallas_call(
        functools.partial(first_kernel, first_slot, slots, size_x, size_y),
        grid=(blocks,),
        in_specs=[smem, smem, pl.BlockSpec((size_x, size_y, LANES), lambda j: (0, 0, half * blocks + j)), whole, whole],
        out_specs=[made, made],
        out_shape=[shape, shape],
        scratch_shapes=[
            pltpu.VMEM((size_x, samples_box), jnp.bfloat16),
            pltpu.VMEM((Q1, samples_box), jnp.float32),
            pltpu.VMEM((Q1, samples_box), jnp.float32),
            pltpu.VMEM((slots, Q, samples_box), jnp.bfloat16),
        ],
        compiler_params=pltpu.CompilerParams(vmem_limit_bytes=VMEM),
        cost_estimate=pl.CostEstimate(
            flops=4 * slots * Q * samples_box * records // 2, bytes_accessed=8 << 20, transcendentals=0
        ),
    )(labels, place, samples, *tables)


def second_kernel(place, kept_ref, came_ref, high_ref, low_ref, out_ref, left_ref):
    side = place[2]
    both = product(high_ref[side], low_ref[side], kept_ref[0] + came_ref[0])
    left_ref[0] = both[:Q]
    out_ref[0] = both[Q:]


def second(place, kept, came, tables):
    slots, _, lanes = kept.shape
    block = pl.BlockSpec((1, Q, lanes), lambda a: (a, 0, 0))
    whole = pl.BlockSpec((2, 2 * Q, Q), lambda a: (0, 0, 0))
    shape = jax.ShapeDtypeStruct(kept.shape, jnp.float32)
    return pl.pallas_call(
        second_kernel,
        grid=(slots,),
        in_specs=[pl.BlockSpec(memory_space=pltpu.SMEM), block, block, whole, whole],
        out_specs=[block, block],
        out_shape=[shape, shape],
        compiler_params=pltpu.CompilerParams(vmem_limit_bytes=VMEM),
        cost_estimate=pl.CostEstimate(
            flops=12 * slots * Q * Q * lanes, bytes_accessed=16 * slots * Q * lanes, transcendentals=0
        ),
    )(place, kept, came, *tables)


def third_kernel(left_a, came_a, left_b, came_b, *rest):
    total_ref = rest[-1]
    lanes = left_a.shape[-1]
    total_ref[0, :, :lanes] = left_a[0] + came_a[0]
    total_ref[0, :, lanes:] = left_b[0] + came_b[0]


def third(total, first_slot, left_a, came_a, left_b, came_b):
    slots, _, lanes = left_a.shape
    block = pl.BlockSpec((1, Q, lanes), lambda a: (a, 0, 0))
    given = [] if total is None else [total]
    return pl.pallas_call(
        third_kernel,
        grid=(slots,),
        in_specs=[block] * 4 + [pl.BlockSpec(memory_space=pl.ANY)] * len(given),
        out_specs=pl.BlockSpec((1, Q, 2 * lanes), lambda a: (first_slot + a, 0, 0)),
        out_shape=jax.ShapeDtypeStruct((FB, Q, 2 * lanes), jnp.float32),
        input_output_aliases={4: 0} if given else {},
        compiler_params=pltpu.CompilerParams(vmem_limit_bytes=VMEM),
        cost_estimate=pl.CostEstimate(
            flops=2 * slots * Q * lanes, bytes_accessed=24 * slots * Q * lanes, transcendentals=0
        ),
    )(left_a, came_a, left_b, came_b, *given)


def swapped(x, axis):
    size = lax.axis_size(axis)
    return lax.ppermute(x, axis, [(i, (i + size // 2) % size) for i in range(size)])


def local(samples, box_labels):
    size_x, size_y, records = samples.shape
    device_x, device_y = lax.axis_index("gx"), lax.axis_index("gy")
    side_x = device_x // (lax.axis_size("gx") // 2)
    side_y = device_y // (lax.axis_size("gy") // 2)
    corner = (device_x * size_x, device_y * size_y)
    place_x = jnp.stack([*corner, side_x]).astype(jnp.int32)
    place_y = jnp.stack([*corner, side_y]).astype(jnp.int32)
    ratio_x = 2.0 * size_x * (N // (2 * size_x)) / N
    ratio_y = 2.0 * size_y * (N // (2 * size_y)) / N
    norm = 1.0 / math.sqrt(size_x * size_y)
    spread_x = lambda g: np.kron(g, np.eye(Q2))
    spread_y = lambda g: np.kron(np.eye(Q1), g)
    first_x = level_tables(Q1, ratio_x, spread_x, norm)
    first_y = level_tables(Q2, ratio_y, spread_y, norm)
    second_x = level_tables(Q1, ratio_x, spread_x, 1.0)
    second_y = level_tables(Q2, ratio_y, spread_y, 1.0)

    starts = [sum(GROUPS[:g]) for g in range(len(GROUPS))]
    ones = []
    for at, slots in zip(starts, GROUPS):
        out_a, kept_a = first(box_labels, place_x, samples, first_x, at, slots, 0)
        came_a = swapped(out_a, "gx")
        out_b, kept_b = first(box_labels, place_y, samples, first_y, at, slots, 1)
        came_b = swapped(out_b, "gy")
        ones.append((kept_a, came_a, kept_b, came_b))
    twos = []
    for kept_a, came_a, kept_b, came_b in ones:
        out_a, left_a = second(place_y, kept_a, came_a, second_y)
        came_a = swapped(out_a, "gy")
        out_b, left_b = second(place_x, kept_b, came_b, second_x)
        came_b = swapped(out_b, "gx")
        twos.append((left_a, came_a, left_b, came_b))
    total = None
    for at, two in zip(starts, twos):
        total = third(total, at, *two)
    return total.reshape(1, 1, FB * Q, records)


def solution(mesh):
    in_specs = (P("gx", "gy", None), P())
    out_specs = P("gx", "gy", None, None)
    return jax.shard_map(local, mesh=mesh, in_specs=in_specs, out_specs=out_specs, check_vma=False)
```

time: 788 us -> 266 us (0.34)
  waiting for transfers between devices: 358 us -> 67.4 us
  other arithmetic: 255 us -> 0.15 us
  Pallas kernels: 0 us -> 138 us
  matrix products: 109 us -> 0 us
  local copies, waits for them, and re-layouts: 48.9 us -> 13.8 us
  starting transfers between devices: 7.43 us -> 41.3 us
    ppermute x2 -> x24, waiting for transfers between devices: 358 us -> 67.4 us  [swapped(): lax.ppermute(x, axis, [(i, (i + size // 2) % size) for i in range(size)])]
    another operation x4 -> x2, other arithmetic: 248 us -> 0.15 us  [the longest x1 0.08 us: local(): place_x = jnp.stack([*corner, side_x]).astype(jnp.int32)]
    pallas_call x0 -> x30, Pallas kernels: none -> 138 us  [the longest x12 100 us: first(): pl.pallas_call(functools.partial(first_kernel, first_slot, slots, size_x,...]
    dot_general x8 -> x0, matrix products: 109 us -> none  [the longest x4 41.9 us: one_group(): return jnp.dot(cas_table, flattened, preferred_element_type=jnp.float32)]
    add x4 -> x0, local copies, waits for them, and re-layouts: 48.2 us -> none  [one_group(): cas_table = (jnp.cos(radians) + jnp.sin(radians)).astype(jnp.bfloat16)]
    ppermute x2 -> x24, starting transfers between devices: 7.43 us -> 41.3 us  [swapped(): lax.ppermute(x, axis, [(i, (i + size // 2) % size) for i in range(size)])]
    unnamed x2 -> x82, local copies, waits for them, and re-layouts: 0.01 us -> 13.8 us
  transfers between devices with their start and end apart: 2 -> 24, of which waited for: 2 -> 9; matrix products, arithmetic and copies ran while one was open for 0% -> 0% of each run, Pallas kernels for 0% -> 51%
where the time goes in v1:
time: 266 us; the launch traced here: 261 us
  Pallas kernels  138 us (52%)
  waiting for transfers between devices  67.4 us (25%)
  starting transfers between devices  41.3 us (16%)
  local copies, waits for them, and re-layouts  13.8 us (5%)
    pallas_call x12, Pallas kernels, first(): pl.pallas_call(functools.partial(first_kernel, first_slot, slots, size_x,...  100 us
    ppermute x24, waiting for transfers between devices, swapped(): lax.ppermute(x, axis, [(i, (i + size // 2) % size) for i in range(size)])  67.4 us
    ppermute x24, starting transfers between devices, swapped(): lax.ppermute(x, axis, [(i, (i + size // 2) % size) for i in range(size)])  41.3 us
    pallas_call x12, Pallas kernels, second(): pl.pallas_call(second_kernel, grid=(slots,), in_specs=[pl.BlockSpec(memor...  27.1 us
    unnamed x82, local copies, waits for them, and re-layouts  13.8 us
    pallas_call x6, Pallas kernels, third(): pl.pallas_call(third_kernel, grid=(slots,), in_specs=[block] * 4 + [pl.Bl...  10.7 us
  transfers between devices with their start and end apart: 24, of which 9 were waited for; matrix products, arithmetic and copies ran while one was open for 0% of the time, Pallas kernels for 51%

profile of v1, /device:TPU:1, one launch (start us, length us, event | category | flops | bytes accessed | tf_op | source)
XLA Modules:
  0.0 261.0 jit_solution(1630253233251968961)
XLA Ops:
  2.5 4.1 %shard_map.120 = (f32[1,128,512]{2,1,0:T(8,128)S(1)}, f32[1,128,512]{2,1,0:T(8,128)S(1)}) custom-call(s32[16]{0:T(128)S(1)} %copy-done.38, s32[3]{0:T(128)S(1)} %pad_add_fusion.2.place, bf16[64,64,1024]{2,1,0:T(8,128)(2,1)} %x_ref.23, bf16[2,256,128]{2,1,0:T(8,128)(2,1)S(1)} %copy-done.6, bf16[2,256,128]{2,1,0:T(8,128)(2,1)S(1)} %copy-done.8), custom_call_target="tpu_custom_call" | custom-call | flops 1073741824 | bytes 8388608 | tf_op jit(solution)/shard_map/pallas_call | solution.py:126
  6.6 3.8 %collective-permute-start.20 = (f32[1,128,512]{2,1,0:T(8,128)S(1)}, f32[1,128,512]{2,1,0:T(8,128)S(1)}, u32[]{:S(2)}, u32[]{:S(2)}) collective-permute-start(f32[1,128,512]{2,1,0:T(8,128)S(1)} %get-tuple-element.94), channel_id=1, source_target_pairs={{0,64},{16,80},{32,96},{48,112},{64,0},{80,16},{96,32},{112,48},{1... | collective-permute-start | bytes 786440 | tf_op jit(solution)/shard_map/ppermute | solution.py:197
  10.6 4.2 %shard_map.122 = (f32[1,128,512]{2,1,0:T(8,128)S(1)}, f32[1,128,512]{2,1,0:T(8,128)S(1)}) custom-call(s32[16]{0:T(128)S(1)} %copy-done.39, s32[3]{0:T(128)S(1)} %pad_add_fusion.place, bf16[64,64,1024]{2,1,0:T(8,128)(2,1)} %x_ref.23, bf16[2,256,128]{2,1,0:T(8,128)(2,1)S(1)} %copy-done.4, bf16[2,256,128]{2,1,0:T(8,128)(2,1)S(1)} %copy-done.5), custom_call_target="tpu_custom_call" | custom-call | flops 1073741824 | bytes 8388608 | tf_op jit(solution)/shard_map/pallas_call | solution.py:126
  14.8 3.7 %collective-permute-start.22 = (f32[1,128,512]{2,1,0:T(8,128)S(1)}, f32[1,128,512]{2,1,0:T(8,128)S(1)}, u32[]{:S(2)}, u32[]{:S(2)}) collective-permute-start(f32[1,128,512]{2,1,0:T(8,128)S(1)} %get-tuple-element.98), channel_id=1, source_target_pairs={{0,8},{1,9},{2,10},{3,11},{4,12},{5,13},{6,14},{7,15},{8,0},{9,1},... | collective-permute-start | bytes 786440 | tf_op jit(solution)/shard_map/ppermute | solution.py:197
  18.4 6.5 %shard_map.116 = (f32[2,128,512]{2,1,0:T(8,128)S(1)}, f32[2,128,512]{2,1,0:T(8,128)S(1)}) custom-call(s32[16]{0:T(128)S(1)} %copy-done.39, s32[3]{0:T(128)S(1)} %pad_add_fusion.2.place, bf16[64,64,1024]{2,1,0:T(8,128)(2,1)} %x_ref.23, bf16[2,256,128]{2,1,0:T(8,128)(2,1)S(1)} %copy-done.7, bf16[2,256,128]{2,1,0:T(8,128)(2,1)S(1)} %copy-done.9), custom_call_target="tpu_custom_call" | custom-call | flops 2147483648 | bytes 8388608 | tf_op jit(solution)/shard_map/pallas_call | solution.py:126
  25.1 4.1 %shard_map.102 = (f32[1,128,512]{2,1,0:T(8,128)S(1)}, f32[1,128,512]{2,1,0:T(8,128)S(1)}) custom-call(s32[16]{0:T(128)S(1)} %copy-done.39, s32[3]{0:T(128)S(1)} %pad_add_fusion.place, bf16[64,64,1024]{2,1,0:T(8,128)(2,1)} %x_ref.23, bf16[2,256,128]{2,1,0:T(8,128)(2,1)S(1)} %copy-done.4, bf16[2,256,128]{2,1,0:T(8,128)(2,1)S(1)} %copy-done.5), custom_call_target="tpu_custom_call" | custom-call | flops 1073741824 | bytes 8388608 | tf_op jit(solution)/shard_map/pallas_call | solution.py:126
  29.9 4.0 %shard_map.100 = (f32[1,128,512]{2,1,0:T(8,128)S(1)}, f32[1,128,512]{2,1,0:T(8,128)S(1)}) custom-call(s32[16]{0:T(128)S(1)} %copy-done.39, s32[3]{0:T(128)S(1)} %pad_add_fusion.2.place, bf16[64,64,1024]{2,1,0:T(8,128)(2,1)} %x_ref.23, bf16[2,256,128]{2,1,0:T(8,128)(2,1)S(1)} %copy-done.7, bf16[2,256,128]{2,1,0:T(8,128)(2,1)S(1)} %copy-done.9), custom_call_target="tpu_custom_call" | custom-call | flops 1073741824 | bytes 8388608 | tf_op jit(solution)/shard_map/pallas_call | solution.py:126
  37.6 14.4 %shard_map.108 = (f32[5,128,512]{2,1,0:T(8,128)}, f32[5,128,512]{2,1,0:T(8,128)S(1)}) custom-call(s32[16]{0:T(128)S(1)} %copy-done.39, s32[3]{0:T(128)S(1)} %pad_add_fusion.2.place, bf16[64,64,1024]{2,1,0:T(8,128)(2,1)} %x_ref.23, bf16[2,256,128]{2,1,0:T(8,128)(2,1)S(1)} %copy-done.7, bf16[2,256,128]{2,1,0:T(8,128)(2,1)S(1)} %copy-done.9), custom_call_target="tpu_custom_call" | custom-call | flops 5368709120 | bytes 8388608 | tf_op jit(solution)/shard_map/pallas_call | solution.py:126
  52.0 14.5 %shard_map.110 = (f32[5,128,512]{2,1,0:T(8,128)}, f32[5,128,512]{2,1,0:T(8,128)S(1)}) custom-call(s32[16]{0:T(128)S(1)} %copy-done.39, s32[3]{0:T(128)S(1)} %pad_add_fusion.place, bf16[64,64,1024]{2,1,0:T(8,128)(2,1)} %x_ref.23, bf16[2,256,128]{2,1,0:T(8,128)(2,1)S(1)} %copy-done.4, bf16[2,256,128]{2,1,0:T(8,128)(2,1)S(1)} %copy-done.5), custom_call_target="tpu_custom_call" | custom-call | flops 5368709120 | bytes 8388608 | tf_op jit(solution)/shard_map/pallas_call | solution.py:126
  72.8 12.0 %shard_map.112 = (f32[4,128,512]{2,1,0:T(8,128)}, f32[4,128,512]{2,1,0:T(8,128)S(1)}) custom-call(s32[16]{0:T(128)S(1)} %copy-done.39, s32[3]{0:T(128)S(1)} %pad_add_fusion.2.place, bf16[64,64,1024]{2,1,0:T(8,128)(2,1)} %x_ref.23, bf16[2,256,128]{2,1,0:T(8,128)(2,1)S(1)} %copy-done.7, bf16[2,256,128]{2,1,0:T(8,128)(2,1)S(1)} %copy-done.9), custom_call_target="tpu_custom_call" | custom-call | flops 4294967296 | bytes 8388608 | tf_op jit(solution)/shard_map/pallas_call | solution.py:126
  89.1 6.5 %shard_map.118 = (f32[2,128,512]{2,1,0:T(8,128)S(1)}, f32[2,128,512]{2,1,0:T(8,128)S(1)}) custom-call(s32[16]{0:T(128)S(1)} %copy-done.39, s32[3]{0:T(128)S(1)} %pad_add_fusion.place, bf16[64,64,1024]{2,1,0:T(8,128)(2,1)} %x_ref.23, bf16[2,256,128]{2,1,0:T(8,128)(2,1)S(1)} %copy-done.4, bf16[2,256,128]{2,1,0:T(8,128)(2,1)S(1)} %copy-done.5), custom_call_target="tpu_custom_call" | custom-call | flops 2147483648 | bytes 8388608 | tf_op jit(solution)/shard_map/pallas_call | solution.py:126
  98.7 8.9 %shard_map.104 = (f32[3,128,512]{2,1,0:T(8,128)S(1)}, f32[3,128,512]{2,1,0:T(8,128)S(1)}) custom-call(s32[16]{0:T(128)S(1)} %copy-done.39, s32[3]{0:T(128)S(1)} %pad_add_fusion.2.place, bf16[64,64,1024]{2,1,0:T(8,128)(2,1)} %x_ref.23, bf16[2,256,128]{2,1,0:T(8,128)(2,1)S(1)} %copy-done.7, bf16[2,256,128]{2,1,0:T(8,128)(2,1)S(1)} %copy-done.9), custom_call_target="tpu_custom_call" | custom-call | flops 3221225472 | bytes 8388608 | tf_op jit(solution)/shard_map/pallas_call | solution.py:126
  110.7 12.0 %shard_map.114 = (f32[4,128,512]{2,1,0:T(8,128)}, f32[4,128,512]{2,1,0:T(8,128)S(1)}) custom-call(s32[16]{0:T(128)S(1)} %copy-done.39, s32[3]{0:T(128)S(1)} %pad_add_fusion.place, bf16[64,64,1024]{2,1,0:T(8,128)(2,1)} %x_ref.23, bf16[2,256,128]{2,1,0:T(8,128)(2,1)S(1)} %copy-done.4, bf16[2,256,128]{2,1,0:T(8,128)(2,1)S(1)} %copy-done.5), custom_call_target="tpu_custom_call" | custom-call | flops 4294967296 | bytes 8388608 | tf_op jit(solution)/shard_map/pallas_call | solution.py:126
  122.9 8.9 %shard_map.106 = (f32[3,128,512]{2,1,0:T(8,128)S(1)}, f32[3,128,512]{2,1,0:T(8,128)S(1)}) custom-call(s32[16]{0:T(128)S(1)} %copy-done.39, s32[3]{0:T(128)S(1)} %pad_add_fusion.place, bf16[64,64,1024]{2,1,0:T(8,128)(2,1)} %x_ref.23, bf16[2,256,128]{2,1,0:T(8,128)(2,1)S(1)} %copy-done.4, bf16[2,256,128]{2,1,0:T(8,128)(2,1)S(1)} %copy-done.5), custom_call_target="tpu_custom_call" | custom-call | flops 3221225472 | bytes 8388608 | tf_op jit(solution)/shard_map/pallas_call | solution.py:126
  139.3 14.9 %collective-permute-done.4.came_ref = f32[3,128,512]{2,1,0:T(8,128)} collective-permute-done((f32[3,128,512]{2,1,0:T(8,128)S(1)}, f32[3,128,512]{2,1,0:T(8,128)}, u32[]{:S(2)}, u32[]{:S(2)}) %collective-permute-start.4) | collective-permute-done | bytes 786464 | tf_op jit(solution)/shard_map/ppermute | solution.py:197
  157.2 3.8 %shard_map.109 = (f32[5,128,512]{2,1,0:T(8,128)}, f32[5,128,512]{2,1,0:T(8,128)S(1)}) custom-call(s32[3]{0:T(128)S(1)} %pad_add_fusion.place, f32[5,128,512]{2,1,0:T(8,128)S(1)} %get-tuple-element.69.kept_ref, f32[5,128,512]{2,1,0:T(8,128)S(1)} %collective-permute-done.8.came_ref, bf16[2,256,128]{2,1,0:T(8,128)(2,1)S(1)} %copy-done, ...), custom_call_target="tpu_custom_call" | custom-call | flops 503316480 | bytes 5242880 | tf_op jit(solution)/shard_map/pallas_call | solution.py:157
  164.2 3.8 %shard_map.111 = (f32[5,128,512]{2,1,0:T(8,128)}, f32[5,128,512]{2,1,0:T(8,128)S(1)}) custom-call(s32[3]{0:T(128)S(1)} %pad_add_fusion.2.place, f32[5,128,512]{2,1,0:T(8,128)S(1)} %get-tuple-element.73.kept_ref, f32[5,128,512]{2,1,0:T(8,128)S(1)} %collective-permute-done.10.came_ref, bf16[2,256,128]{2,1,0:T(8,128)(2,1)S(1)} %copy-done.2, ...), custom_call_target="tpu_custom_call" | custom-call | flops 503316480 | bytes 5242880 | tf_op jit(solution)/shard_map/pallas_call | solution.py:157
  168.0 7.0 %collective-permute-done.6.came_ref = f32[3,128,512]{2,1,0:T(8,128)} collective-permute-done((f32[3,128,512]{2,1,0:T(8,128)S(1)}, f32[3,128,512]{2,1,0:T(8,128)}, u32[]{:S(2)}, u32[]{:S(2)}) %collective-permute-start.6) | collective-permute-done | bytes 786464 | tf_op jit(solution)/shard_map/ppermute | solution.py:197
  181.1 5.1 %collective-permute-done.17.came_a = f32[2,128,512]{2,1,0:T(8,128)} collective-permute-done((f32[2,128,512]{2,1,0:T(8,128)S(1)}, f32[2,128,512]{2,1,0:T(8,128)}, u32[]{:S(2)}, u32[]{:S(2)}) %collective-permute-start.17) | collective-permute-done | bytes 524320 | tf_op jit(solution)/shard_map/ppermute | solution.py:197
  192.8 3.6 %shard_map.107 = (f32[3,128,512]{2,1,0:T(8,128)}, f32[3,128,512]{2,1,0:T(8,128)S(1)}) custom-call(s32[3]{0:T(128)S(1)} %pad_add_fusion.2.place, f32[3,128,512]{2,1,0:T(8,128)S(1)} %copy-done.11, f32[3,128,512]{2,1,0:T(8,128)} %collective-permute-done.6.came_ref, bf16[2,256,128]{2,1,0:T(8,128)(2,1)S(1)} %copy-done.2, bf16[2,256,128]{2,1,0:T(8,128)(2,1)S(1)} %copy-done.3), custom_call_target="tpu_custom_call" | custom-call | flops 301989888 | bytes 3145728 | tf_op jit(solution)/shard_map/pallas_call | solution.py:157
  197.5 11.1 %collective-permute-done.13.came_a = f32[4,128,512]{2,1,0:T(8,128)S(1)} collective-permute-done((f32[4,128,512]{2,1,0:T(8,128)}, f32[4,128,512]{2,1,0:T(8,128)S(1)}, u32[]{:S(2)}, u32[]{:S(2)}) %collective-permute-start.13) | collective-permute-done | bytes 1048608 | tf_op jit(solution)/shard_map/ppermute | solution.py:197
  215.3 17.6 %collective-permute-done.15.came_b = f32[4,128,512]{2,1,0:T(8,128)S(1)} collective-permute-done((f32[4,128,512]{2,1,0:T(8,128)}, f32[4,128,512]{2,1,0:T(8,128)S(1)}, u32[]{:S(2)}, u32[]{:S(2)}) %collective-permute-start.15) | collective-permute-done | bytes 1048608 | tf_op jit(solution)/shard_map/ppermute | solution.py:197
  246.9 6.7 %collective-permute-done.5.came_a = f32[3,128,512]{2,1,0:T(8,128)S(1)} collective-permute-done((f32[3,128,512]{2,1,0:T(8,128)}, f32[3,128,512]{2,1,0:T(8,128)S(1)}, u32[]{:S(2)}, u32[]{:S(2)}) %collective-permute-start.5) | collective-permute-done | bytes 786464 | tf_op jit(solution)/shard_map/ppermute | solution.py:197
  255.4 3.8 %collective-permute-done.1.came_a = f32[1,128,512]{2,1,0:T(8,128)} collective-permute-done((f32[1,128,512]{2,1,0:T(8,128)S(1)}, f32[1,128,512]{2,1,0:T(8,128)}, u32[]{:S(2)}, u32[]{:S(2)}) %collective-permute-start.1) | collective-permute-done | bytes 262176 | tf_op jit(solution)/shard_map/ppermute | solution.py:197
  (138 shorter events, 75.5 us)
Async XLA Ops:
  6.6 59.9 %collective-permute-start.20 = (f32[1,128,512]{2,1,0:T(8,128)S(1)}, f32[1,128,512]{2,1,0:T(8,128)S(1)}, u32[]{:S(2)}, u32[]{:S(2)}) collective-permute-start(f32[1,128,512]{2,1,0:T(8,128)S(1)} %get-tuple-element.94), channel_id=1, source_target_pairs={{0,64},{16,80},{32,96},{48,112},{64,0},{80,16},{96,32},{112,48},{1... | collective-permute-start | bytes 786440 | tf_op jit(solution)/shard_map/ppermute | solution.py:197
  14.8 56.3 %collective-permute-start.22 = (f32[1,128,512]{2,1,0:T(8,128)S(1)}, f32[1,128,512]{2,1,0:T(8,128)S(1)}, u32[]{:S(2)}, u32[]{:S(2)}) collective-permute-start(f32[1,128,512]{2,1,0:T(8,128)S(1)} %get-tuple-element.98), channel_id=1, source_target_pairs={{0,8},{1,9},{2,10},{3,11},{4,12},{5,13},{6,14},{7,15},{8,0},{9,1},... | collective-permute-start | bytes 786440 | tf_op jit(solution)/shard_map/ppermute | solution.py:197
  25.0 82.7 %collective-permute-start.16 = (f32[2,128,512]{2,1,0:T(8,128)S(1)}, f32[2,128,512]{2,1,0:T(8,128)S(1)}, u32[]{:S(2)}, u32[]{:S(2)}) collective-permute-start(f32[2,128,512]{2,1,0:T(8,128)S(1)} %get-tuple-element.86), channel_id=1, source_target_pairs={{0,64},{16,80},{32,96},{48,112},{64,0},{80,16},{96,32},{112,48},{1... | collective-permute-start | bytes 1572872 | tf_op jit(solution)/shard_map/ppermute | solution.py:197
  29.9 54.9 %collective-permute-start.2 = (f32[1,128,512]{2,1,0:T(8,128)S(1)}, f32[1,128,512]{2,1,0:T(8,128)S(1)}, u32[]{:S(2)}, u32[]{:S(2)}) collective-permute-start(f32[1,128,512]{2,1,0:T(8,128)S(1)} %get-tuple-element.58), channel_id=1, source_target_pairs={{0,8},{1,9},{2,10},{3,11},{4,12},{5,13},{6,14},{7,15},{8,0},{9,1},... | collective-permute-start | bytes 786440 | tf_op jit(solution)/shard_map/ppermute | solution.py:197
  34.7 53.7 %collective-permute-start = (f32[1,128,512]{2,1,0:T(8,128)S(1)}, f32[1,128,512]{2,1,0:T(8,128)S(1)}, u32[]{:S(2)}, u32[]{:S(2)}) collective-permute-start(f32[1,128,512]{2,1,0:T(8,128)S(1)} %get-tuple-element.54), channel_id=1, source_target_pairs={{0,64},{16,80},{32,96},{48,112},{64,0},{80,16},{96,32},{112,48},{1... | collective-permute-start | bytes 786440 | tf_op jit(solution)/shard_map/ppermute | solution.py:197
  68.1 27.5 %collective-permute-start.21 = (f32[1,128,512]{2,1,0:T(8,128)S(1)}, f32[1,128,512]{2,1,0:T(8,128)S(1)}, u32[]{:S(2)}, u32[]{:S(2)}) collective-permute-start(f32[1,128,512]{2,1,0:T(8,128)S(1)} %get-tuple-element.96), channel_id=1, source_target_pairs={{0,8},{1,9},{2,10},{3,11},{4,12},{5,13},{6,14},{7,15},{8,0},{9,1},... | collective-permute-start | bytes 786440 | tf_op jit(solution)/shard_map/ppermute | solution.py:197
  72.7 23.1 %collective-permute-start.23 = (f32[1,128,512]{2,1,0:T(8,128)S(1)}, f32[1,128,512]{2,1,0:T(8,128)S(1)}, u32[]{:S(2)}, u32[]{:S(2)}) collective-permute-start(f32[1,128,512]{2,1,0:T(8,128)S(1)} %get-tuple-element.100), channel_id=1, source_target_pairs={{0,64},{16,80},{32,96},{48,112},{64,0},{80,16},{96,32},{112,48},{1... | collective-permute-start | bytes 786440 | tf_op jit(solution)/shard_map/ppermute | solution.py:197
  85.4 46.4 %collective-permute-start.12 = (f32[4,128,512]{2,1,0:T(8,128)}, f32[4,128,512]{2,1,0:T(8,128)S(1)}, u32[]{:S(2)}, u32[]{:S(2)}) collective-permute-start(f32[4,128,512]{2,1,0:T(8,128)} %get-tuple-element.78), channel_id=1, source_target_pairs={{0,64},{16,80},{32,96},{48,112},{64,0},{80,16},{96,32},{112,48},{1... | collective-permute-start | bytes 3145736 | tf_op jit(solution)/shard_map/ppermute | solution.py:197
  89.1 65.5 %collective-permute-start.8 = (f32[5,128,512]{2,1,0:T(8,128)}, f32[5,128,512]{2,1,0:T(8,128)S(1)}, u32[]{:S(2)}, u32[]{:S(2)}) collective-permute-start(f32[5,128,512]{2,1,0:T(8,128)} %get-tuple-element.70), channel_id=1, source_target_pairs={{0,64},{16,80},{32,96},{48,112},{64,0},{80,16},{96,32},{112,48},{1... | collective-permute-start | bytes 3932168 | tf_op jit(solution)/shard_map/ppermute | solution.py:197
  95.7 27.0 %collective-permute-start.18 = (f32[2,128,512]{2,1,0:T(8,128)S(1)}, f32[2,128,512]{2,1,0:T(8,128)S(1)}, u32[]{:S(2)}, u32[]{:S(2)}) collective-permute-start(f32[2,128,512]{2,1,0:T(8,128)S(1)} %get-tuple-element.90), channel_id=1, source_target_pairs={{0,8},{1,9},{2,10},{3,11},{4,12},{5,13},{6,14},{7,15},{8,0},{9,1},... | collective-permute-start | bytes 1572872 | tf_op jit(solution)/shard_map/ppermute | solution.py:197
  95.8 65.2 %collective-permute-start.10 = (f32[5,128,512]{2,1,0:T(8,128)}, f32[5,128,512]{2,1,0:T(8,128)S(1)}, u32[]{:S(2)}, u32[]{:S(2)}) collective-permute-start(f32[5,128,512]{2,1,0:T(8,128)} %get-tuple-element.74), channel_id=1, source_target_pairs={{0,8},{1,9},{2,10},{3,11},{4,12},{5,13},{6,14},{7,15},{8,0},{9,1},... | collective-permute-start | bytes 3932168 | tf_op jit(solution)/shard_map/ppermute | solution.py:197
  107.7 46.5 %collective-permute-start.4 = (f32[3,128,512]{2,1,0:T(8,128)S(1)}, f32[3,128,512]{2,1,0:T(8,128)}, u32[]{:S(2)}, u32[]{:S(2)}) collective-permute-start(f32[3,128,512]{2,1,0:T(8,128)S(1)} %get-tuple-element.62), channel_id=1, source_target_pairs={{0,64},{16,80},{32,96},{48,112},{64,0},{80,16},{96,32},{112,48},{1... | collective-permute-start | bytes 2359304 | tf_op jit(solution)/shard_map/ppermute | solution.py:197
  122.7 55.2 %collective-permute-start.14 = (f32[4,128,512]{2,1,0:T(8,128)}, f32[4,128,512]{2,1,0:T(8,128)S(1)}, u32[]{:S(2)}, u32[]{:S(2)}) collective-permute-start(f32[4,128,512]{2,1,0:T(8,128)} %get-tuple-element.82), channel_id=1, source_target_pairs={{0,8},{1,9},{2,10},{3,11},{4,12},{5,13},{6,14},{7,15},{8,0},{9,1},... | collective-permute-start | bytes 3145736 | tf_op jit(solution)/shard_map/ppermute | solution.py:197
  131.9 43.2 %collective-permute-start.6 = (f32[3,128,512]{2,1,0:T(8,128)S(1)}, f32[3,128,512]{2,1,0:T(8,128)}, u32[]{:S(2)}, u32[]{:S(2)}) collective-permute-start(f32[3,128,512]{2,1,0:T(8,128)S(1)} %get-tuple-element.66), channel_id=1, source_target_pairs={{0,8},{1,9},{2,10},{3,11},{4,12},{5,13},{6,14},{7,15},{8,0},{9,1},... | collective-permute-start | bytes 2359304 | tf_op jit(solution)/shard_map/ppermute | solution.py:197
  154.2 32.0 %collective-permute-start.17 = (f32[2,128,512]{2,1,0:T(8,128)S(1)}, f32[2,128,512]{2,1,0:T(8,128)}, u32[]{:S(2)}, u32[]{:S(2)}) collective-permute-start(f32[2,128,512]{2,1,0:T(8,128)S(1)} %get-tuple-element.88), channel_id=1, source_target_pairs={{0,8},{1,9},{2,10},{3,11},{4,12},{5,13},{6,14},{7,15},{8,0},{9,1},... | collective-permute-start | bytes 1572872 | tf_op jit(solution)/shard_map/ppermute | solution.py:197
  154.5 54.1 %collective-permute-start.13 = (f32[4,128,512]{2,1,0:T(8,128)}, f32[4,128,512]{2,1,0:T(8,128)S(1)}, u32[]{:S(2)}, u32[]{:S(2)}) collective-permute-start(f32[4,128,512]{2,1,0:T(8,128)} %get-tuple-element.80), channel_id=1, source_target_pairs={{0,8},{1,9},{2,10},{3,11},{4,12},{5,13},{6,14},{7,15},{8,0},{9,1},... | collective-permute-start | bytes 3145736 | tf_op jit(solution)/shard_map/ppermute | solution.py:197
  161.0 75.7 %collective-permute-start.9 = (f32[5,128,512]{2,1,0:T(8,128)}, f32[5,128,512]{2,1,0:T(8,128)S(1)}, u32[]{:S(2)}, u32[]{:S(2)}) collective-permute-start(f32[5,128,512]{2,1,0:T(8,128)} %get-tuple-element.72), channel_id=1, source_target_pairs={{0,8},{1,9},{2,10},{3,11},{4,12},{5,13},{6,14},{7,15},{8,0},{9,1},... | collective-permute-start | bytes 3932168 | tf_op jit(solution)/shard_map/ppermute | solution.py:197
  175.0 21.4 %collective-permute-start.19 = (f32[2,128,512]{2,1,0:T(8,128)}, f32[2,128,512]{2,1,0:T(8,128)S(1)}, u32[]{:S(2)}, u32[]{:S(2)}) collective-permute-start(f32[2,128,512]{2,1,0:T(8,128)} %get-tuple-element.92), channel_id=1, source_target_pairs={{0,64},{16,80},{32,96},{48,112},{64,0},{80,16},{96,32},{112,48},{1... | collective-permute-start | bytes 1572872 | tf_op jit(solution)/shard_map/ppermute | solution.py:197
  177.9 66.4 %collective-permute-start.11 = (f32[5,128,512]{2,1,0:T(8,128)}, f32[5,128,512]{2,1,0:T(8,128)S(1)}, u32[]{:S(2)}, u32[]{:S(2)}) collective-permute-start(f32[5,128,512]{2,1,0:T(8,128)} %get-tuple-element.76), channel_id=1, source_target_pairs={{0,64},{16,80},{32,96},{48,112},{64,0},{80,16},{96,32},{112,48},{1... | collective-permute-start | bytes 3932168 | tf_op jit(solution)/shard_map/ppermute | solution.py:197
  186.3 46.6 %collective-permute-start.15 = (f32[4,128,512]{2,1,0:T(8,128)}, f32[4,128,512]{2,1,0:T(8,128)S(1)}, u32[]{:S(2)}, u32[]{:S(2)}) collective-permute-start(f32[4,128,512]{2,1,0:T(8,128)} %get-tuple-element.84), channel_id=1, source_target_pairs={{0,64},{16,80},{32,96},{48,112},{64,0},{80,16},{96,32},{112,48},{1... | collective-permute-start | bytes 3145736 | tf_op jit(solution)/shard_map/ppermute | solution.py:197
  197.2 56.4 %collective-permute-start.5 = (f32[3,128,512]{2,1,0:T(8,128)}, f32[3,128,512]{2,1,0:T(8,128)S(1)}, u32[]{:S(2)}, u32[]{:S(2)}) collective-permute-start(f32[3,128,512]{2,1,0:T(8,128)} %copy-done.40), channel_id=1, source_target_pairs={{0,8},{1,9},{2,10},{3,11},{4,12},{5,13},{6,14},{7,15},{8,0},{9,1},... | collective-permute-start | bytes 2359304 | tf_op jit(solution)/shard_map/ppermute | solution.py:197
  208.6 44.9 %collective-permute-start.7 = (f32[3,128,512]{2,1,0:T(8,128)}, f32[3,128,512]{2,1,0:T(8,128)S(1)}, u32[]{:S(2)}, u32[]{:S(2)}) collective-permute-start(f32[3,128,512]{2,1,0:T(8,128)} %get-tuple-element.68), channel_id=1, source_target_pairs={{0,64},{16,80},{32,96},{48,112},{64,0},{80,16},{96,32},{112,48},{1... | collective-permute-start | bytes 2359304 | tf_op jit(solution)/shard_map/ppermute | solution.py:197
  232.9 22.5 %collective-permute-start.3 = (f32[1,128,512]{2,1,0:T(8,128)S(1)}, f32[1,128,512]{2,1,0:T(8,128)S(1)}, u32[]{:S(2)}, u32[]{:S(2)}) collective-permute-start(f32[1,128,512]{2,1,0:T(8,128)S(1)} %get-tuple-element.60), channel_id=1, source_target_pairs={{0,64},{16,80},{32,96},{48,112},{64,0},{80,16},{96,32},{112,48},{1... | collective-permute-start | bytes 786440 | tf_op jit(solution)/shard_map/ppermute | solution.py:197
  236.7 22.5 %collective-permute-start.1 = (f32[1,128,512]{2,1,0:T(8,128)S(1)}, f32[1,128,512]{2,1,0:T(8,128)}, u32[]{:S(2)}, u32[]{:S(2)}) collective-permute-start(f32[1,128,512]{2,1,0:T(8,128)S(1)} %get-tuple-element.56), channel_id=1, source_target_pairs={{0,8},{1,9},{2,10},{3,11},{4,12},{5,13},{6,14},{7,15},{8,0},{9,1},... | collective-permute-start | bytes 786440 | tf_op jit(solution)/shard_map/ppermute | solution.py:197
  (41 other events, 336.2 us)

commit v2 on v0

v2 whole, which is shorter than its diff:
```python
import functools
import math

import jax
import jax.numpy as jnp
import numpy as np
from jax import lax
from jax.experimental import pallas as pl
from jax.experimental.pallas import tpu as pltpu
from jax.sharding import PartitionSpec as P

N = 16384
FBY = 4
FB = 16
Q1 = 8
Q2 = 16
Q = Q1 * Q2
LANES = 256
MESH = pl.DeviceIdType.MESH


def cheb_nodes(points):
    return np.cos(np.pi * (2.0 * np.arange(points) + 1.0) / (2.0 * points))


def level_matrix(points, box_ratio, side, child):
    nodes = cheb_nodes(points)
    targets = child - 0.5 + 0.5 * nodes
    weights = np.ones((points, points))
    for m in range(points):
        for other in range(points):
            if other != m:
                weights[:, m] *= (targets - nodes[other]) / (nodes[m] - nodes[other])
    turns = ((child - 0.5) * 0.5 + 0.25 * nodes[:, None] - 0.5 * nodes[None, :]) * (box_ratio * (side - 0.5) * 0.5)
    radians = 2.0 * np.pi * turns
    return weights * (np.cos(radians) + np.sin(radians))


def level_tables(points, box_ratio, spread):
    both = np.stack(
        [
            np.concatenate([spread(level_matrix(points, box_ratio, s, c)) for c in (s, 1 - s)], axis=0)
            for s in (0, 1)
        ]
    ).astype(np.float32)
    high = both.astype(jnp.bfloat16)
    low = (both - high.astype(np.float32)).astype(jnp.bfloat16)
    return np.stack([high, low], axis=1)


def product(tables, value):
    high, low = tables[0], tables[1]
    value_high = value.astype(jnp.bfloat16)
    value_low = (value - value_high.astype(jnp.float32)).astype(jnp.bfloat16)
    dot = functools.partial(jnp.dot, preferred_element_type=jnp.float32)
    return dot(high, value_high) + (dot(low, value_high) + dot(high, value_low))


def node_column(points):
    counter = lax.broadcasted_iota(jnp.int32, (points, 1), 0).astype(jnp.float32)
    return jnp.cos(jnp.pi * (2.0 * counter + 1.0) / (2.0 * points))


def kernel(
    labels, samples, level_consts, total,
    x_ref, levels, spread, wide, table, sent, came, last,
    x_sem, level_sem, send_sem, came_sem, resend_sem, last_sem,
):
    size_x, size_y, records = samples.shape
    samples_box = size_x * size_y
    width_x, width_y = N // (2 * size_x), N // (2 * size_y)
    norm = 1.0 / math.sqrt(samples_box)
    half = records // 2
    blocks = records // LANES
    count_x, count_y = lax.axis_size("gx"), lax.axis_size("gy")
    device_x, device_y = lax.axis_index("gx"), lax.axis_index("gy")
    partners = (
        (lax.rem(device_x + count_x // 2, count_x), device_y),
        (device_x, lax.rem(device_y + count_y // 2, count_y)),
    )
    sides = (device_x // (count_x // 2), device_y // (count_y // 2))

    barrier = pltpu.get_barrier_semaphore()
    for partner in partners:
        pl.semaphore_signal(barrier, inc=1, device_id=partner, device_id_type=MESH)

    def load_block(j):
        lanes = pl.ds(j * LANES, LANES)
        return pltpu.make_async_copy(samples.at[:, :, lanes], x_ref.at[:, :, lanes], x_sem.at[j])

    def load_level(axis):
        return pltpu.make_async_copy(level_consts.at[axis, sides[axis]], levels.at[axis], level_sem.at[axis])

    load_block(0).start()
    for axis in range(2):
        load_level(axis).start()
    for j in range(1, blocks):
        load_block(j).start()

    owner = lax.broadcasted_iota(jnp.int32, (size_x, samples_box), 1) // size_y
    row = lax.broadcasted_iota(jnp.int32, (size_x, samples_box), 0)
    spread[...] = (owner == row).astype(jnp.float32).astype(jnp.bfloat16)
    steps_x = lax.broadcasted_iota(jnp.int32, (Q1, size_x), 1).astype(jnp.float32)
    steps_y = (lax.broadcasted_iota(jnp.int32, (Q2, 2 * size_y), 1) % size_y).astype(jnp.float32)
    nodes_x, nodes_y = node_column(Q1), node_column(Q2)

    def build_table(slot):
        label = labels[slot]
        centre_x = (label // FBY) * width_x + width_x // 2
        centre_y = (label % FBY) * width_y + width_y // 2
        corner = ((device_x * size_x * centre_x + device_y * size_y * centre_y) % N).astype(jnp.float32)
        points_x = centre_x.astype(jnp.float32) + 0.5 * width_x * nodes_x
        points_y = centre_y.astype(jnp.float32) + 0.5 * width_y * nodes_y
        angle_x = 2.0 * jnp.pi * ((corner + points_x * steps_x) / N)
        angle_y = 2.0 * jnp.pi * ((points_y * steps_y) / N)
        cos_y, sin_y = jnp.cos(angle_y), jnp.sin(angle_y)
        plus_y, minus_y = cos_y + sin_y, cos_y - sin_y
        parts = jnp.concatenate([jnp.cos(angle_x), jnp.sin(angle_x)], axis=0)
        parts_high = parts.astype(jnp.bfloat16).astype(jnp.float32)
        stacked = jnp.concatenate([parts_high, parts - parts_high], axis=0).astype(jnp.bfloat16)
        expanded = jnp.dot(stacked, spread[...], preferred_element_type=jnp.float32)
        wide[...] = expanded[: 2 * Q1] + expanded[2 * Q1 :]
        pair = 2 * size_y
        run = 4 * pair

        def fill(step, _):
            for i in range(Q1):
                for at in range(0, run, pair):
                    lanes = pl.ds(pl.multiple_of(step * run, run) + at, pair)
                    cos_x, sin_x = wide[i : i + 1, lanes], wide[Q1 + i : Q1 + i + 1, lanes]
                    table[i * Q2 : (i + 1) * Q2, lanes] = (cos_x * plus_y + sin_x * minus_y).astype(jnp.bfloat16)
            return 0

        lax.fori_loop(0, samples_box // run, fill, 0)

    def send(axis, slot):
        return pltpu.make_async_remote_copy(
            src_ref=sent.at[axis, slot], dst_ref=came.at[axis, slot],
            send_sem=send_sem.at[axis, slot], recv_sem=came_sem.at[axis, slot],
            device_id=partners[axis], device_id_type=MESH,
        )

    def resend(axis, slot):
        return pltpu.make_async_remote_copy(
            src_ref=came.at[axis, slot], dst_ref=last.at[axis, slot],
            send_sem=resend_sem.at[axis, slot], recv_sem=last_sem.at[axis, slot],
            device_id=partners[1 - axis], device_id_type=MESH,
        )

    def first(slot, _):
        build_table(slot)
        for j in range(blocks):
            axis = j // (blocks // 2)

            @pl.when(slot == 0)
            def _(j=j, axis=axis):
                load_block(j).wait()
                if j % (blocks // 2) == 0:
                    load_level(axis).wait()

            lanes = slice(j * LANES, (j + 1) * LANES)
            within = slice(j * LANES - axis * half, (j + 1) * LANES - axis * half)
            block = x_ref[:, :, lanes].reshape(samples_box, LANES)
            initial = norm * jnp.dot(table[...], block, preferred_element_type=jnp.float32)
            both = product(levels.at[axis], initial)
            total[slot, :, lanes] = both[:Q]
            sent[axis, slot, :, within] = both[Q:]
            if j % (blocks // 2) == blocks // 2 - 1:
                if axis == 0:

                    @pl.when(slot == 0)
                    def _():
                        pl.semaphore_wait(barrier, 2)

                send(axis, slot).start()
        return 0

    lax.fori_loop(0, FB, first, 0)

    def second(slot, _):
        for axis in range(2):
            lanes = slice(axis * half, (axis + 1) * half)
            send(axis, slot).wait_recv()
            both = product(levels.at[1 - axis], total[slot, :, lanes] + came[axis, slot])
            total[slot, :, lanes] = both[:Q]
            came[axis, slot] = both[Q:]
            resend(axis, slot).start()
        return 0

    lax.fori_loop(0, FB, second, 0)

    def third(slot, _):
        for axis in range(2):
            lanes = slice(axis * half, (axis + 1) * half)
            send(axis, slot).wait_send()
            resend(axis, slot).wait()
            total[slot, :, lanes] += last[axis, slot]
        return 0

    lax.fori_loop(0, FB, third, 0)


def local(samples, box_labels):
    size_x, size_y, records = samples.shape
    ratio_x = 2.0 * size_x * (N // (2 * size_x)) / N
    ratio_y = 2.0 * size_y * (N // (2 * size_y)) / N
    consts = np.stack(
        [
            level_tables(Q1, ratio_x, lambda g: np.kron(g, np.eye(Q2))),
            level_tables(Q2, ratio_y, lambda g: np.kron(np.eye(Q1), g)),
        ]
    )
    half = records // 2
    held = pltpu.VMEM((2, FB, Q, half), jnp.float32)
    sems = pltpu.SemaphoreType.DMA((2, FB))
    total = pl.pallas_call(
        kernel,
        in_specs=[
            pl.BlockSpec(memory_space=pltpu.SMEM),
            pl.BlockSpec(memory_space=pl.ANY),
            pl.BlockSpec(memory_space=pl.ANY),
        ],
        out_specs=pl.BlockSpec(memory_space=pltpu.VMEM),
        out_shape=pltpu.VMEM((FB, Q, records), jnp.float32),
        scratch_shapes=[
            pltpu.VMEM(samples.shape, jnp.bfloat16),
            pltpu.VMEM((2, 2, 2 * Q, Q), jnp.bfloat16),
            pltpu.VMEM((size_x, size_x * size_y), jnp.bfloat16),
            pltpu.VMEM((2 * Q1, size_x * size_y), jnp.float32),
            pltpu.VMEM((Q, size_x * size_y), jnp.bfloat16),
            held, held, held,
            pltpu.SemaphoreType.DMA((records // LANES,)),
            pltpu.SemaphoreType.DMA((2,)),
            sems, sems, sems, sems,
        ],
        compiler_params=pltpu.CompilerParams(collective_id=0, has_side_effects=True, vmem_limit_bytes=46 << 20),
    )(box_labels, samples, jnp.asarray(consts))
    return total.reshape(1, 1, FB * Q, records)


def solution(mesh):
    in_specs = (P("gx", "gy", None), P())
    out_specs = P("gx", "gy", None, None)
    return jax.shard_map(local, mesh=mesh, in_specs=in_specs, out_specs=out_specs, check_vma=False)
```

time: 788 us -> 196 us (0.25); the launches traced: 779 us -> 196 us
  waiting for transfers between devices: 358 us -> 0 us
  other arithmetic: 255 us -> 0 us
  Pallas kernels: 0 us -> 193 us
  matrix products: 109 us -> 0 us
  local copies, waits for them, and re-layouts: 48.9 us -> 3.4 us
    ppermute x2 -> x0, waiting for transfers between devices: 358 us -> none  [swapped(): lax.ppermute(x, axis, [(i, i ^ 1 << distance) for i in range(lax.axis_siz...]
    another operation x4 -> x0, other arithmetic: 248 us -> none
    pallas_call x0 -> x1, Pallas kernels: none -> 193 us  [local(): pl.pallas_call(kernel, in_specs=[pl.BlockSpec(memory_space=pltpu.SMEM), p...]
    dot_general x8 -> x0, matrix products: 109 us -> none  [the longest x4 41.9 us: one_group(): return jnp.dot(cas_table, flattened, preferred_element_type=jnp.float32)]
    add x4 -> x0, local copies, waits for them, and re-layouts: 48.2 us -> none  [one_group(): cas_table = (jnp.cos(radians) + jnp.sin(radians)).astype(jnp.bfloat16)]
  transfers between devices with their start and end apart: 2 -> 0, of which waited for: 2 -> 0; matrix products, arithmetic and copies ran while one was open for 0% -> 0% of each run, Pallas kernels for 0% -> 0%
where the time goes in v2:
time: 196 us
  Pallas kernels  193 us (98%)
  local copies, waits for them, and re-layouts  3.4 us (2%)
    pallas_call x1, Pallas kernels, local(): pl.pallas_call(kernel, in_specs=[pl.BlockSpec(memory_space=pltpu.SMEM), p...  193 us

profile of v2, /device:TPU:1, one launch (start us, length us, event | category | flops | bytes accessed | tf_op | source)
XLA Modules:
  0.0 196.2 jit_solution(16970062355077768604)
XLA Ops:
  0.0 192.8 %shard_map.37 = f32[16,128,1024]{2,1,0:T(8,128)S(1)} custom-call(s32[16]{0:T(128)} %labels.1, bf16[64,64,1024]{2,1,0:T(8,128)(2,1)} %samples.1, bf16[2,2,2,256,128]{4,3,2,1,0:T(8,128)(2,1)} %constant.2.clone.level_consts), custom_call_target="tpu_custom_call" | custom-call | tf_op jit(solution)/shard_map/pallas_call | solution.py:216
  192.8 3.4 %copy.5 = f32[1,1,2048,1024]{3,2,1,0:T(8,128)} copy(f32[1,1,2048,1024]{3,2,1,0:T(8,128)S(1)} %bitcast.1) | data formatting | bytes 16777216

commit v3 on v2

v3 whole, which is shorter than its diff:
```python
import functools
import math

import jax
import jax.numpy as jnp
import numpy as np
from jax import lax
from jax.experimental import pallas as pl
from jax.experimental.pallas import tpu as pltpu
from jax.sharding import PartitionSpec as P

N = 16384
FBY = 4
FB = 16
Q1 = 8
Q2 = 16
Q = Q1 * Q2
LANES = 512
FINE = 256
MESH = pl.DeviceIdType.MESH
SENDS = ((1, 1), (2, 1), (3, 1), (4, 1), (5, 1), (6, 1), (7, 1), (8, 1), (9, 1), (10, 1), (11, 1), (12, 1), (13, 1), (14, 1), (15, 1))
RESENDS = ((0, 1), (1, 1), (2, 1), (3, 1), (4, 1), (5, 1), (6, 1), (7, 1), (8, 1), (9, 1), (10, 1), (11, 1), (12, 1), (13, 1), (14, 1), (15, 1))
FLIGHT = 16


def cheb_nodes(points):
    return np.cos(np.pi * (2.0 * np.arange(points) + 1.0) / (2.0 * points))


def level_matrix(points, box_ratio, side, child):
    nodes = cheb_nodes(points)
    targets = child - 0.5 + 0.5 * nodes
    weights = np.ones((points, points))
    for m in range(points):
        for other in range(points):
            if other != m:
                weights[:, m] *= (targets - nodes[other]) / (nodes[m] - nodes[other])
    turns = ((child - 0.5) * 0.5 + 0.25 * nodes[:, None] - 0.5 * nodes[None, :]) * (box_ratio * (side - 0.5) * 0.5)
    radians = 2.0 * np.pi * turns
    return weights * (np.cos(radians) + np.sin(radians))


def level_tables(points, box_ratio, spread):
    both = np.stack(
        [
            np.concatenate([spread(level_matrix(points, box_ratio, s, c)) for c in (s, 1 - s)], axis=0)
            for s in (0, 1)
        ]
    ).astype(np.float32)
    high = both.astype(jnp.bfloat16)
    low = (both - high.astype(np.float32)).astype(jnp.bfloat16)
    return np.stack([high, low], axis=1)


def product(tables, value):
    high, low = tables[0], tables[1]
    value_high = value.astype(jnp.bfloat16)
    value_low = (value - value_high.astype(jnp.float32)).astype(jnp.bfloat16)
    dot = functools.partial(jnp.dot, preferred_element_type=jnp.float32)
    return dot(high, value_high) + (dot(low, value_high) + dot(high, value_low))


def kernel(
    labels_in, samples, level_consts, total,
    labels, x_ref, levels, spread, wide, narrow, table, sent, came, last,
    label_sem, x_sem, level_sem, send_sem, came_sem, resend_sem, last_sem,
):
    size_x, size_y, records = samples.shape
    samples_box = size_x * size_y
    width_x, width_y = N // (2 * size_x), N // (2 * size_y)
    norm = 1.0 / math.sqrt(samples_box)
    half = records // 2
    blocks, fine = records // LANES, records // FINE
    count_x, count_y = lax.axis_size("gx"), lax.axis_size("gy")
    device_x, device_y = lax.axis_index("gx"), lax.axis_index("gy")
    partners = (
        (lax.rem(device_x + count_x // 2, count_x), device_y),
        (device_x, lax.rem(device_y + count_y // 2, count_y)),
    )
    sides = (device_x // (count_x // 2), device_y // (count_y // 2))
    order = [axis * (fine // 2) + k for k in range(fine // 2) for axis in (1, 0)]

    barrier = pltpu.get_barrier_semaphore()
    for partner in partners:
        pl.semaphore_signal(barrier, inc=1, device_id=partner, device_id_type=MESH)

    def load_block(j):
        lanes = pl.ds(j * FINE, FINE)
        return pltpu.make_async_copy(samples.at[:, :, lanes], x_ref.at[:, :, lanes], x_sem.at[j])

    def load_level(axis):
        return pltpu.make_async_copy(level_consts.at[axis, sides[axis]], levels.at[axis], level_sem.at[axis])

    load_labels = pltpu.make_async_copy(labels_in, labels, label_sem)
    load_labels.start()
    load_block(order[0]).start()
    for axis in range(2):
        load_level(axis).start()
    for j in order[1:]:
        load_block(j).start()

    boxes_x = FB // FBY
    column = lax.broadcasted_iota(jnp.int32, (size_x, samples_box), 1)
    first_column = size_y * lax.broadcasted_iota(jnp.int32, (size_x, samples_box), 0)
    inside = (column >= first_column) & (column < first_column + size_y)
    spread[...] = jnp.where(inside, 1.0, 0.0).astype(jnp.bfloat16)
    row = lax.broadcasted_iota(jnp.int32, (boxes_x * Q1, 1), 0)
    centre = (row // Q1) * width_x + width_x // 2
    node = jnp.cos(jnp.pi * (2.0 * (row % Q1).astype(jnp.float32) + 1.0) / (2.0 * Q1))
    corner = ((device_x * size_x * centre) % N).astype(jnp.float32)
    step = lax.broadcasted_iota(jnp.int32, (boxes_x * Q1, size_x), 1).astype(jnp.float32)
    angle = 2.0 * jnp.pi * ((corner + (centre.astype(jnp.float32) + 0.5 * width_x * node) * step) / N)
    parts = jnp.concatenate([jnp.cos(angle), jnp.sin(angle)], axis=0)
    parts_high = parts.astype(jnp.bfloat16).astype(jnp.float32)
    for k, part in enumerate((parts_high, parts - parts_high)):
        repeated = jnp.dot(part.astype(jnp.bfloat16), spread[...], preferred_element_type=jnp.float32)
        repeated = repeated.reshape(2, boxes_x, Q1, samples_box)
        if k == 0:
            wide[...] = repeated
        else:
            wide[...] += repeated

    row = lax.broadcasted_iota(jnp.int32, (FBY * Q2, 1), 0)
    centre = (row // Q2) * width_y + width_y // 2
    node = jnp.cos(jnp.pi * (2.0 * (row % Q2).astype(jnp.float32) + 1.0) / (2.0 * Q2))
    corner = ((device_y * size_y * centre) % N).astype(jnp.float32)
    step = (lax.broadcasted_iota(jnp.int32, (FBY * Q2, 2 * size_y), 1) % size_y).astype(jnp.float32)
    angle = 2.0 * jnp.pi * ((corner + (centre.astype(jnp.float32) + 0.5 * width_y * node) * step) / N)
    narrow[0] = (jnp.cos(angle) + jnp.sin(angle)).reshape(FBY, Q2, 2 * size_y)
    narrow[1] = (jnp.cos(angle) - jnp.sin(angle)).reshape(FBY, Q2, 2 * size_y)
    load_labels.wait()

    def build_table(slot):
        label_x, label_y = labels[slot] // FBY, labels[slot] % FBY
        plus_y, minus_y = narrow[0, label_y], narrow[1, label_y]
        pair = 2 * size_y
        run = 4 * pair

        def fill(k, _):
            for i in range(Q1):
                for at in range(0, run, pair):
                    lanes = pl.ds(pl.multiple_of(k * run, run) + at, pair)
                    cos_x, sin_x = wide[0, label_x, i : i + 1, lanes], wide[1, label_x, i : i + 1, lanes]
                    table[i * Q2 : (i + 1) * Q2, lanes] = (cos_x * plus_y + sin_x * minus_y).astype(jnp.bfloat16)
            return 0

        lax.fori_loop(0, samples_box // run, fill, 0)

    whole = [(start, slots, 0, half) for start, slots in SENDS]
    pieces = [(0, 1, at, FINE) for at in range(0, half, FINE)]
    sends = pieces + whole
    resends = [(start, slots, 0, half) for start, slots in RESENDS]

    def view(ref, axis, message):
        start, slots, at, width = message
        return ref.at[axis, pl.ds(start, slots), :, pl.ds(at, width)]

    def send(axis, k):
        return pltpu.make_async_remote_copy(
            src_ref=view(sent, axis, sends[k]), dst_ref=view(came, axis, sends[k]),
            send_sem=send_sem.at[axis, k], recv_sem=came_sem.at[axis, k],
            device_id=partners[axis], device_id_type=MESH,
        )

    def resend(axis, k):
        return pltpu.make_async_remote_copy(
            src_ref=view(came, axis, resends[k]), dst_ref=view(last, axis, resends[k]),
            send_sem=resend_sem.at[axis, k], recv_sem=last_sem.at[axis, k],
            device_id=partners[1 - axis], device_id_type=MESH,
        )

    def at_end(messages, slot, act, skip=0):
        for k, (start, slots, _, _) in enumerate(messages):
            if k >= skip:
                pl.when(slot == start + slots - 1)(functools.partial(act, k))

    def at_start(messages, slot, act):
        for k, (start, _, _, _) in enumerate(messages):
            pl.when(slot == start)(functools.partial(act, k))

    def start_send(axis, k):
        if k >= FLIGHT:
            send(axis, k - FLIGHT).wait_send()
        send(axis, k).start()

    def start_resend(axis, k):
        if k >= FLIGHT:
            resend(axis, k - FLIGHT).wait_send()
        else:
            send(1 - axis, len(sends) + k - FLIGHT).wait_send()
        resend(axis, k).start()

    def first_level(axis, slot, at, width):
        lanes = slice(axis * half + at, axis * half + at + width)
        block = x_ref[:, :, lanes].reshape(samples_box, width)
        initial = norm * jnp.dot(table[...], block, preferred_element_type=jnp.float32)
        both = product(levels.at[axis], initial)
        total[slot, :, lanes] = both[:Q]
        sent[axis, slot, :, at : at + width] = both[Q:]

    build_table(0)
    for at, j in enumerate(order):
        axis, k = j // (fine // 2), j % (fine // 2)
        load_block(j).wait()
        if at < 2:
            load_level(axis).wait()
        first_level(axis, 0, k * FINE, FINE)
        if at == 0:
            pl.semaphore_wait(barrier, 2)
        start_send(axis, k)

    def first(slot, _):
        build_table(slot)
        for axis in (1, 0):
            for at in range(0, half, LANES):
                first_level(axis, slot, at, LANES)
            at_end(sends, slot, functools.partial(start_send, axis), len(pieces))
        return 0

    lax.fori_loop(1, FB, first, 0)

    def second(slot, _):
        for axis in (1, 0):
            lanes = slice(axis * half, (axis + 1) * half)
            at_start(sends, slot, lambda k, axis=axis: send(axis, k).wait_recv())
            both = product(levels.at[1 - axis], total[slot, :, lanes] + came[axis, slot])
            total[slot, :, lanes] = both[:Q]
            came[axis, slot] = both[Q:]
            at_end(resends, slot, functools.partial(start_resend, axis))
        return 0

    lax.fori_loop(0, FB, second, 0)

    def third(slot, _):
        for axis in (1, 0):
            lanes = slice(axis * half, (axis + 1) * half)
            at_start(resends, slot, lambda k, axis=axis: resend(axis, k).wait_recv())
            total[slot, :, lanes] += last[axis, slot]
        return 0

    lax.fori_loop(0, FB, third, 0)
    for axis in (1, 0):
        for k in range(len(resends) - FLIGHT, len(resends)):
            resend(axis, k).wait_send()


def local(samples, box_labels):
    size_x, size_y, records = samples.shape
    ratio_x = 2.0 * size_x * (N // (2 * size_x)) / N
    ratio_y = 2.0 * size_y * (N // (2 * size_y)) / N
    consts = np.stack(
        [
            level_tables(Q1, ratio_x, lambda g: np.kron(g, np.eye(Q2))),
            level_tables(Q2, ratio_y, lambda g: np.kron(np.eye(Q1), g)),
        ]
    )
    half = records // 2
    held = pltpu.VMEM((2, FB, Q, half), jnp.float32)
    sems = pltpu.SemaphoreType.DMA((2, FB + half // FINE))
    total = pl.pallas_call(
        kernel,
        in_specs=[
            pl.BlockSpec(memory_space=pl.ANY),
            pl.BlockSpec(memory_space=pl.ANY),
            pl.BlockSpec(memory_space=pl.ANY),
        ],
        out_specs=pl.BlockSpec(memory_space=pltpu.VMEM),
        out_shape=pltpu.VMEM((FB, Q, records), jnp.float32),
        scratch_shapes=[
            pltpu.SMEM(box_labels.shape, jnp.int32),
            pltpu.VMEM(samples.shape, jnp.bfloat16),
            pltpu.VMEM((2, 2, 2 * Q, Q), jnp.bfloat16),
            pltpu.VMEM((size_x, size_x * size_y), jnp.bfloat16),
            pltpu.VMEM((2, FB // FBY, Q1, size_x * size_y), jnp.float32),
            pltpu.VMEM((2, FBY, Q2, 2 * size_y), jnp.float32),
            pltpu.VMEM((Q, size_x * size_y), jnp.bfloat16),
            held, held, held,
            pltpu.SemaphoreType.DMA,
            pltpu.SemaphoreType.DMA((records // FINE,)),
            pltpu.SemaphoreType.DMA((2,)),
            sems, sems, sems, sems,
        ],
        compiler_params=pltpu.CompilerParams(collective_id=0, has_side_effects=True, vmem_limit_bytes=46 << 20),
    )(box_labels, samples, jnp.asarray(consts))
    return total.reshape(1, 1, FB * Q, records)


def solution(mesh):
    in_specs = (P("gx", "gy", None), P())
    out_specs = P("gx", "gy", None, None)
    return jax.shard_map(local, mesh=mesh, in_specs=in_specs, out_specs=out_specs, check_vma=False)
```

time: 196 us -> 194 us (0.990)
  Pallas kernels: 193 us -> 190 us
    pallas_call x1, Pallas kernels: 193 us -> 190 us  [local(): pl.pallas_call(kernel, in_specs=[pl.BlockSpec(memory_space=pl.ANY), pl.Bl...]
where the time goes in v3:
time: 194 us
  Pallas kernels  190 us (98%)
  local copies, waits for them, and re-layouts  3.4 us (2%)
    pallas_call x1, Pallas kernels, local(): pl.pallas_call(kernel, in_specs=[pl.BlockSpec(memory_space=pl.ANY), pl.Bl...  190 us

profile of v3, /device:TPU:1, one launch (start us, length us, event | category | flops | bytes accessed | tf_op | source)
XLA Modules:
  0.0 193.8 jit_solution(15862769684021364121)
XLA Ops:
  0.0 190.3 %shard_map.37 = f32[16,128,1024]{2,1,0:T(8,128)S(1)} custom-call(s32[16]{0:T(128)} %labels_in.1, bf16[64,64,1024]{2,1,0:T(8,128)(2,1)} %samples.1, bf16[2,2,2,256,128]{4,3,2,1,0:T(8,128)(2,1)} %constant.2.clone.level_consts), custom_call_target="tpu_custom_call" | custom-call | tf_op jit(solution)/shard_map/pallas_call | solution.py:260
  190.4 3.4 %copy.5 = f32[1,1,2048,1024]{3,2,1,0:T(8,128)} copy(f32[1,1,2048,1024]{3,2,1,0:T(8,128)S(1)} %bitcast.1) | data formatting | bytes 16777216

commit v4 on v3

--- a/solution.py
+++ b/solution.py
@@ -18,9 +18,8 @@
 LANES = 512
 FINE = 256
 MESH = pl.DeviceIdType.MESH
-SENDS = ((1, 1), (2, 1), (3, 1), (4, 1), (5, 1), (6, 1), (7, 1), (8, 1), (9, 1), (10, 1), (11, 1), (12, 1), (13, 1), (14, 1), (15, 1))
-RESENDS = ((0, 1), (1, 1), (2, 1), (3, 1), (4, 1), (5, 1), (6, 1), (7, 1), (8, 1), (9, 1), (10, 1), (11, 1), (12, 1), (13, 1), (14, 1), (15, 1))
-FLIGHT = 16
+SENDS = ((1, 1), (2, 1), (3, 1), (4, 2), (6, 2), (8, 4), (12, 4))
+RESENDS = ((0, 2), (2, 2), (4, 4), (8, 4), (12, 2), (14, 1), (15, 1))
 
 
 def cheb_nodes(points):
@@ -89,7 +88,7 @@
         return pltpu.make_async_copy(samples.at[:, :, lanes], x_ref.at[:, :, lanes], x_sem.at[j])
 
     def load_level(axis):
-        return pltpu.make_async_copy(level_consts.at[axis, sides[axis]], levels.at[axis], level_sem.at[axis])
+        return pltpu.make_async_copy(level_consts.at[axis, sides[axis]], levels.at[axis], level_sem)
 
     load_labels = pltpu.make_async_copy(labels_in, labels, label_sem)
     load_labels.start()
@@ -158,14 +157,14 @@
     def send(axis, k):
         return pltpu.make_async_remote_copy(
             src_ref=view(sent, axis, sends[k]), dst_ref=view(came, axis, sends[k]),
-            send_sem=send_sem.at[axis, k], recv_sem=came_sem.at[axis, k],
+            send_sem=send_sem.at[axis], recv_sem=came_sem.at[axis, k],
             device_id=partners[axis], device_id_type=MESH,
         )
 
     def resend(axis, k):
         return pltpu.make_async_remote_copy(
             src_ref=view(came, axis, resends[k]), dst_ref=view(last, axis, resends[k]),
-            send_sem=resend_sem.at[axis, k], recv_sem=last_sem.at[axis, k],
+            send_sem=resend_sem.at[axis], recv_sem=last_sem.at[axis, k],
             device_id=partners[1 - axis], device_id_type=MESH,
         )
 
@@ -177,18 +176,6 @@
     def at_start(messages, slot, act):
         for k, (start, _, _, _) in enumerate(messages):
             pl.when(slot == start)(functools.partial(act, k))
-
-    def start_send(axis, k):
-        if k >= FLIGHT:
-            send(axis, k - FLIGHT).wait_send()
-        send(axis, k).start()
-
-    def start_resend(axis, k):
-        if k >= FLIGHT:
-            resend(axis, k - FLIGHT).wait_send()
-        else:
-            send(1 - axis, len(sends) + k - FLIGHT).wait_send()
-        resend(axis, k).start()
 
     def first_level(axis, slot, at, width):
         lanes = slice(axis * half + at, axis * half + at + width)
@@ -202,19 +189,19 @@
     for at, j in enumerate(order):
         axis, k = j // (fine // 2), j % (fine // 2)
         load_block(j).wait()
-        if at < 2:
-            load_level(axis).wait()
+        if at == 0:
+            pltpu.make_async_copy(level_consts.at[:, 0], levels, level_sem).wait()
         first_level(axis, 0, k * FINE, FINE)
         if at == 0:
             pl.semaphore_wait(barrier, 2)
-        start_send(axis, k)
+        send(axis, k).start()
 
     def first(slot, _):
         build_table(slot)
         for axis in (1, 0):
             for at in range(0, half, LANES):
                 first_level(axis, slot, at, LANES)
-            at_end(sends, slot, functools.partial(start_send, axis), len(pieces))
+            at_end(sends, slot, lambda k, axis=axis: send(axis, k).start(), len(pieces))
         return 0
 
     lax.fori_loop(1, FB, first, 0)
@@ -226,7 +213,7 @@
             both = product(levels.at[1 - axis], total[slot, :, lanes] + came[axis, slot])
             total[slot, :, lanes] = both[:Q]
             came[axis, slot] = both[Q:]
-            at_end(resends, slot, functools.partial(start_resend, axis))
+            at_end(resends, slot, lambda k, axis=axis: resend(axis, k).start())
         return 0
 
     lax.fori_loop(0, FB, second, 0)
@@ -239,9 +226,13 @@
         return 0
 
     lax.fori_loop(0, FB, third, 0)
-    for axis in (1, 0):
-        for k in range(len(resends) - FLIGHT, len(resends)):
-            resend(axis, k).wait_send()
+    for axis in range(2):
+        for source, target, out_sem, in_sem in ((sent, came, send_sem, came_sem), (came, last, resend_sem, last_sem)):
+            pltpu.make_async_remote_copy(
+                src_ref=source.at[axis], dst_ref=target.at[axis],
+                send_sem=out_sem.at[axis], recv_sem=in_sem.at[axis, 0],
+                device_id=partners[axis], device_id_type=MESH,
+            ).wait_send()
 
 
 def local(samples, box_labels):
@@ -256,7 +247,7 @@
     )
     half = records // 2
     held = pltpu.VMEM((2, FB, Q, half), jnp.float32)
-    sems = pltpu.SemaphoreType.DMA((2, FB + half // FINE))
+    pair = pltpu.SemaphoreType.DMA((2,))
     total = pl.pallas_call(
         kernel,
         in_specs=[
@@ -277,8 +268,9 @@
             held, held, held,
             pltpu.SemaphoreType.DMA,
             pltpu.SemaphoreType.DMA((records // FINE,)),
-            pltpu.SemaphoreType.DMA((2,)),
-            sems, sems, sems, sems,
+            pltpu.SemaphoreType.DMA,
+            pair, pltpu.SemaphoreType.DMA((2, half // FINE + len(SENDS))),
+            pair, pltpu.SemaphoreType.DMA((2, len(RESENDS))),
         ],
         compiler_params=pltpu.CompilerParams(collective_id=0, has_side_effects=True, vmem_limit_bytes=46 << 20),
     )(box_labels, samples, jnp.asarray(consts))

time: 194 us -> 193 us (level)
  no operation moved by 1% of the time
where the time goes in v4:
time: 193 us
  Pallas kernels  189 us (98%)
  local copies, waits for them, and re-layouts  3.4 us (2%)
    pallas_call x1, Pallas kernels, local(): pl.pallas_call(kernel, in_specs=[pl.BlockSpec(memory_space=pl.ANY), pl.Bl...  189 us

profile of v4, /device:TPU:1, one launch (start us, length us, event | category | flops | bytes accessed | tf_op | source)
XLA Modules:
  0.0 192.7 jit_solution(1416772003111193595)
XLA Ops:
  0.0 189.3 %shard_map.37 = f32[16,128,1024]{2,1,0:T(8,128)S(1)} custom-call(s32[16]{0:T(128)} %labels_in.1, bf16[64,64,1024]{2,1,0:T(8,128)(2,1)} %samples.1, bf16[2,2,2,256,128]{4,3,2,1,0:T(8,128)(2,1)} %constant.2.clone.level_consts), custom_call_target="tpu_custom_call" | custom-call | tf_op jit(solution)/shard_map/pallas_call | solution.py:251
  189.3 3.4 %copy.5 = f32[1,1,2048,1024]{3,2,1,0:T(8,128)} copy(f32[1,1,2048,1024]{3,2,1,0:T(8,128)S(1)} %bitcast.1) | data formatting | bytes 16777216

commit v5 on v4

--- a/solution.py
+++ b/solution.py
@@ -16,10 +16,10 @@
 Q2 = 16
 Q = Q1 * Q2
 LANES = 512
-FINE = 256
+PIECES = (256, 256)
 MESH = pl.DeviceIdType.MESH
-SENDS = ((1, 1), (2, 1), (3, 1), (4, 2), (6, 2), (8, 4), (12, 4))
-RESENDS = ((0, 2), (2, 2), (4, 4), (8, 4), (12, 2), (14, 1), (15, 1))
+SENDS = ((1, 1), (2, 2), (4, 4), (8, 8))
+RESENDS = ((0, 4), (4, 8), (12, 3), (15, 1))
 
 
 def cheb_nodes(points):
@@ -69,7 +69,6 @@
     width_x, width_y = N // (2 * size_x), N // (2 * size_y)
     norm = 1.0 / math.sqrt(samples_box)
     half = records // 2
-    blocks, fine = records // LANES, records // FINE
     count_x, count_y = lax.axis_size("gx"), lax.axis_size("gy")
     device_x, device_y = lax.axis_index("gx"), lax.axis_index("gy")
     partners = (
@@ -77,14 +76,16 @@
         (device_x, lax.rem(device_y + count_y // 2, count_y)),
     )
     sides = (device_x // (count_x // 2), device_y // (count_y // 2))
-    order = [axis * (fine // 2) + k for k in range(fine // 2) for axis in (1, 0)]
+    starts = [sum(PIECES[:k]) for k in range(len(PIECES))]
+    order = [(axis, at, width) for at, width in zip(starts, PIECES) for axis in (1, 0)]
 
     barrier = pltpu.get_barrier_semaphore()
     for partner in partners:
         pl.semaphore_signal(barrier, inc=1, device_id=partner, device_id_type=MESH)
 
     def load_block(j):
-        lanes = pl.ds(j * FINE, FINE)
+        axis, at, width = order[j]
+        lanes = pl.ds(axis * half + at, width)
         return pltpu.make_async_copy(samples.at[:, :, lanes], x_ref.at[:, :, lanes], x_sem.at[j])
 
     def load_level(axis):
@@ -92,10 +93,10 @@
 
     load_labels = pltpu.make_async_copy(labels_in, labels, label_sem)
     load_labels.start()
-    load_block(order[0]).start()
+    load_block(0).start()
     for axis in range(2):
         load_level(axis).start()
-    for j in order[1:]:
+    for j in range(1, len(order)):
         load_block(j).start()
 
     boxes_x = FB // FBY
@@ -146,7 +147,7 @@
         lax.fori_loop(0, samples_box // run, fill, 0)
 
     whole = [(start, slots, 0, half) for start, slots in SENDS]
-    pieces = [(0, 1, at, FINE) for at in range(0, half, FINE)]
+    pieces = [(0, 1, at, width) for at, width in zip(starts, PIECES)]
     sends = pieces + whole
     resends = [(start, slots, 0, half) for start, slots in RESENDS]
 
@@ -186,15 +187,14 @@
         sent[axis, slot, :, at : at + width] = both[Q:]
 
     build_table(0)
-    for at, j in enumerate(order):
-        axis, k = j // (fine // 2), j % (fine // 2)
+    for j, (axis, at, width) in enumerate(order):
         load_block(j).wait()
-        if at == 0:
+        if j == 0:
             pltpu.make_async_copy(level_consts.at[:, 0], levels, level_sem).wait()
-        first_level(axis, 0, k * FINE, FINE)
-        if at == 0:
+        first_level(axis, 0, at, width)
+        if j == 0:
             pl.semaphore_wait(barrier, 2)
-        send(axis, k).start()
+        send(axis, starts.index(at)).start()
 
     def first(slot, _):
         build_table(slot)
@@ -267,9 +267,9 @@
             pltpu.VMEM((Q, size_x * size_y), jnp.bfloat16),
             held, held, held,
             pltpu.SemaphoreType.DMA,
-            pltpu.SemaphoreType.DMA((records // FINE,)),
+            pltpu.SemaphoreType.DMA((2 * len(PIECES),)),
             pltpu.SemaphoreType.DMA,
-            pair, pltpu.SemaphoreType.DMA((2, half // FINE + len(SENDS))),
+            pair, pltpu.SemaphoreType.DMA((2, len(PIECES) + len(SENDS))),
             pair, pltpu.SemaphoreType.DMA((2, len(RESENDS))),
         ],
         compiler_params=pltpu.CompilerParams(collective_id=0, has_side_effects=True, vmem_limit_bytes=46 << 20),

time: 193 us -> 193 us (level)
  no operation moved by 1% of the time
where the time goes in v5:
time: 193 us
  Pallas kernels  189 us (98%)
  local copies, waits for them, and re-layouts  3.4 us (2%)
    pallas_call x1, Pallas kernels, local(): pl.pallas_call(kernel, in_specs=[pl.BlockSpec(memory_space=pl.ANY), pl.Bl...  189 us

profile of v5, /device:TPU:1, one launch (start us, length us, event | category | flops | bytes accessed | tf_op | source)
XLA Modules:
  0.0 192.6 jit_solution(15037337931743242586)
XLA Ops:
  0.0 189.2 %shard_map.37 = f32[16,128,1024]{2,1,0:T(8,128)S(1)} custom-call(s32[16]{0:T(128)} %labels_in.1, bf16[64,64,1024]{2,1,0:T(8,128)(2,1)} %samples.1, bf16[2,2,2,256,128]{4,3,2,1,0:T(8,128)(2,1)} %constant.2.clone.level_consts), custom_call_target="tpu_custom_call" | custom-call | tf_op jit(solution)/shard_map/pallas_call | solution.py:251
  189.2 3.4 %copy.5 = f32[1,1,2048,1024]{3,2,1,0:T(8,128)} copy(f32[1,1,2048,1024]{3,2,1,0:T(8,128)S(1)} %bitcast.1) | data formatting | bytes 16777216

commit v6 on v5

--- a/solution.py
+++ b/solution.py
@@ -16,7 +16,7 @@
 Q2 = 16
 Q = Q1 * Q2
 LANES = 512
-PIECES = (256, 256)
+PIECES = (128, 128, 256)
 MESH = pl.DeviceIdType.MESH
 SENDS = ((1, 1), (2, 2), (4, 4), (8, 8))
 RESENDS = ((0, 4), (4, 8), (12, 3), (15, 1))

time: 193 us -> 193 us (level)
  no operation moved by 1% of the time
where the time goes in v6:
time: 193 us
  Pallas kernels  189 us (98%)
  local copies, waits for them, and re-layouts  3.4 us (2%)
    pallas_call x1, Pallas kernels, local(): pl.pallas_call(kernel, in_specs=[pl.BlockSpec(memory_space=pl.ANY), pl.Bl...  189 us

profile of v6, /device:TPU:1, one launch (start us, length us, event | category | flops | bytes accessed | tf_op | source)
XLA Modules:
  0.0 192.7 jit_solution(5201034364216603832)
XLA Ops:
  0.0 189.3 %shard_map.37 = f32[16,128,1024]{2,1,0:T(8,128)S(1)} custom-call(s32[16]{0:T(128)} %labels_in.1, bf16[64,64,1024]{2,1,0:T(8,128)(2,1)} %samples.1, bf16[2,2,2,256,128]{4,3,2,1,0:T(8,128)(2,1)} %constant.2.clone.level_consts), custom_call_target="tpu_custom_call" | custom-call | tf_op jit(solution)/shard_map/pallas_call | solution.py:251
  189.3 3.4 %copy.5 = f32[1,1,2048,1024]{3,2,1,0:T(8,128)} copy(f32[1,1,2048,1024]{3,2,1,0:T(8,128)S(1)} %bitcast.1) | data formatting | bytes 16777216
